TPU v7x, 128 devices: a whole 4x4x4 slice. The times are simulated.
128 devices in a mesh: row: 8 (over y, z_hi), col: 16 (over x, z_lo, core).
Axes of the slice: x: 4, y: 4, z: 4 (z_hi: 2, z_lo: 2; z = z_hi * 2 + z_lo), core: 2. Of those that a mesh axis runs over, the one named last changes fastest.
Arguments:
- out_grad: bfloat16 [2048, 16384], P('col', 'row'), may hold values from -6 to 6
- codes: int32 [53248, 8192], P('col', 'row'), may hold values from 0 to 255
- scales: bfloat16 [416, 16384], P('col', 'row'), may hold values from 0.0007972717 to 0.0033874512
- activations: bfloat16 [2048, 53248], P('row', 'col'), may hold values from -6 to 6
- l_ff: bfloat16 [64, 53248], P(None, 'col'), may hold values from 0.099609375 to 1.8984375
- tenant_ids: int32 [2048], P('row'), may hold values from 0 to 63
Outputs:
- input_grad: bfloat16 [2048, 53248], P('row', 'col')
- tenant_grad: float32 [64, 53248], P('row', 'col')
All inputs are finite; a program needn't handle non-finite values.
Results may differ from a plain program's by a relative error of at most 0.02.
Values may be sent and summed in bfloat16 or wider, within the bound.
No kernel may reach another device: no remote copies, remote signals or barrier semaphores. Data moves between devices by JAX's collectives and lax.ppermute only.
A program may use at most 256 MiB of HBM per device.

v0:
```python
import jax
import jax.numpy as jnp
from jax import lax
from jax.sharding import PartitionSpec as P


def unpack(packed):
    low_part = packed % 16
    high_part = packed // 16
    stacked = jnp.stack([low_part - 8, high_part - 8], axis=-1)
    return stacked.reshape(packed.shape[0], packed.shape[1] * 2)


def dequantize(packed, group_scales):
    values = unpack(packed).astype(jnp.float32)
    n_rows, n_cols = values.shape
    n_groups = group_scales.shape[0]
    scaled = (
        values.reshape(n_groups, n_rows // n_groups, n_cols)
        * group_scales.astype(jnp.float32)[:, None, :]
    )
    return scaled.reshape(n_rows, n_cols).astype(jnp.bfloat16)


def project(panel_rows, weight):
    return lax.dot_general(
        panel_rows, weight, (((1,), (1,)), ((), ())), preferred_element_type=jnp.float32
    )


def per_device(out_grad, codes, scales, activations, l_ff, tenant_ids):
    weight = dequantize(codes, scales)
    terms = project(lax.all_gather(out_grad, "col", axis=0, tiled=True), weight)
    gradient = lax.psum_scatter(
        terms.astype(jnp.bfloat16), "row", scatter_dimension=0, tiled=True
    ).astype(jnp.float32)
    onehot = tenant_ids[:, None] == jnp.arange(l_ff.shape[0], dtype=jnp.int32)[None, :]
    gains = jnp.dot(onehot.astype(jnp.bfloat16), l_ff, preferred_element_type=jnp.float32)
    input_grad = (gradient * gains).astype(jnp.bfloat16)
    product = gradient * activations.astype(jnp.float32)
    tenant_terms = jnp.dot(
        onehot.astype(jnp.float32).T,
        product,
        precision=lax.Precision.HIGHEST,
        preferred_element_type=jnp.float32,
    )
    tenant_grad = lax.psum_scatter(
        tenant_terms.astype(jnp.bfloat16), "row", scatter_dimension=0, tiled=True
    ).astype(jnp.float32)
    return (input_grad, tenant_grad)


def solution(mesh):
    in_specs = (
        P("col", "row"),
        P("col", "row"),
        P("col", "row"),
        P("row", "col"),
        P(None, "col"),
        P("row"),
    )
    out_specs = (P("row", "col"), P("row", "col"))
    return jax.shard_map(
        per_device, mesh=mesh, in_specs=in_specs, out_specs=out_specs, check_vma=False
    )
```

profile of v0, /device:TPU:0, one launch (start us, length us, event | category | flops | bytes accessed | tf_op | source)
XLA Modules:
  0.0 420.2 jit_solution(17631610306818768954)
XLA Ops:
  7.2 0.0 copy-start
  7.2 0.0 all-gather.2.cloned.1.call-start
  7.2 0.7 all-gather.2.cloned.1.call-update
  7.9 0.0 reduce-scatter.3.cloned.1.call-start
  8.0 14.3 %fusion.1 = (s32[3328,1024,1]{1,0,2:T(8,128)S(1)}, s32[3328,1024,1]{1,0,2:T(8,128)S(1)}) fusion(s32[3328,1024]{1,0:T(8,128)} %param.7), kind=kLoop, calls=%fused_computation.9 | loop fusion | flops 71565312 | bytes 40894464 | tf_op jit(solution)/shard_map/stack | solution.py:10
  22.2 9.6 %add_convert_fusion = f32[3328,1024,2]{1,0,2:T(8,128)} fusion(s32[3328,1024,1]{1,0,2:T(8,128)S(1)} %get-tuple-element.9, s32[3328,1024,1]{1,0,2:T(8,128)S(1)} %get-tuple-element.8), kind=kLoop, calls=%fused_computation | loop fusion | flops 13631488 | bytes 54525952 | tf_op jit(solution)/shard_map/convert_element_type | solution.py:15
  31.8 40.4 %copy.16 = f32[3328,1024,2]{0,2,1:T(2,128)} copy(f32[3328,1024,2]{1,0,2:T(8,128)} %add_convert_fusion) | data formatting | bytes 54525952 | tf_op jit(solution)/shard_map/convert_element_type | solution.py:15
  72.2 0.0 copy-start.1
  72.2 32.5 %convert_element_type.38 = f32[3328,2048]{0,1:T(8,128)} reshape(f32[3328,1024,2]{0,2,1:T(2,128)} %copy.16) | data formatting | bytes 54525952 | tf_op jit(solution)/shard_map/convert_element_type | solution.py:15
  104.8 0.0 copy-done.1
  104.8 12.5 %mul.17 = f32[26,128,2048]{2,1,0:T(8,128)} broadcast(bf16[26,2048]{1,0:T(8,128)(2,1)S(1)} %copy-done.1), dimensions={0,2} | broadcast | bytes 27369472 | tf_op jit(solution)/shard_map/mul | solution.py:19
  117.3 25.5 %copy.17 = f32[3328,2048]{0,1:T(8,128)} copy(f32[3328,2048]{1,0:T(8,128)} %bitcast.11) | data formatting | bytes 54525952 | tf_op jit(solution)/shard_map/mul | solution.py:19
  142.8 0.0 all-gather.2.cloned.1.call-done
  142.8 39.6 %fusion.5 = bf16[2048,3328]{0,1:T(8,128)(2,1)} fusion(bf16[2048,2048]{1,0:T(8,128)(2,1)} %all-gather.2.cloned.1.call-done, f32[3328,2048]{0,1:T(8,128)} %convert_element_type.38, f32[3328,2048]{0,1:T(8,128)} %copy.17), kind=kOutput, calls=%fused_computation.14 | convolution fusion | flops 27937734656 | bytes 76546048 | tf_op jit(solution)/shard_map/dot_general | solution.py:26
  182.3 0.0 copy-start.2
  182.3 0.0 reduce-scatter.3.cloned.1.call-update
  182.4 0.2 reduce-scatter.5.cloned.1.call-start
  182.6 2.8 copy.19
  185.4 160.4 %reduce-scatter.3.cloned.1.call-done = bf16[256,3328]{0,1:T(8,128)(2,1)} async-done(((bf16[2048,3328]{0,1:T(8,128)(2,1)}), bf16[256,3328]{0,1:T(8,128)(2,1)}) %reduce-scatter.3.cloned.1.call-update) | async-done | bytes 1703952 | tf_op jit(solution)/shard_map/reduce_scatter | solution.py:34
  345.7 0.0 copy-done.2
  345.7 4.4 %convolution_convert_fusion.1 = bf16[64,3328]{1,0:T(8,128)(2,1)} fusion(bf16[256,3328]{0,1:T(8,128)(2,1)} %reduce-scatter.3.cloned.1.call-done, bf16[256,3328]{0,1:T(8,128)(2,1)S(1)} %copy.19, s32[256]{0:T(256)S(1)} %copy-done.2), kind=kOutput, calls=%fused_computation.18 | convolution fusion | flops 657113088 | bytes 3834880 | tf_op jit(solution)/shard_map/dot_general | solution.py:41
  350.1 0.0 reduce-scatter.5.cloned.1.call-update
  350.2 0.0 copy-done
  350.2 2.2 fusion.7
  352.3 2.4 copy.20
  354.7 57.5 %reduce-scatter.5.cloned.1.call-done = bf16[8,3328]{1,0:T(8,128)(2,1)} async-done(((bf16[64,3328]{1,0:T(8,128)(2,1)}), bf16[8,3328]{1,0:T(8,128)(2,1)}) %reduce-scatter.5.cloned.1.call-update) | async-done | bytes 53264 | tf_op jit(solution)/shard_map/reduce_scatter | solution.py:47
  412.2 1.5 convert_element_type.47
Async XLA Ops:
  7.2 343.0 %copy-start = (bf16[64,3328]{1,0:T(8,128)(2,1)S(1)}, bf16[64,3328]{1,0:T(8,128)(2,1)}, u32[]{:S(2)}) copy-start(bf16[64,3328]{1,0:T(8,128)(2,1)} %param.10) | copy-start | bytes 1277956
  7.2 135.6 %all-gather.2.cloned.1.call-start = ((), (), s32[]{:S(2)}) async-start(), calls=%async_computation.2 | async-start | bytes 8912896 | tf_op jit(solution)/shard_map/all_gather | solution.py:33
  7.9 337.8 %reduce-scatter.3.cloned.1.call-start = ((), (), s32[]{:S(2)}) async-start(), calls=%async_computation.3 | async-start | bytes 15335424 | tf_op jit(solution)/shard_map/reduce_scatter | solution.py:34
  72.2 32.5 %copy-start.1 = (bf16[26,2048]{1,0:T(8,128)(2,1)S(1)}, bf16[26,2048]{1,0:T(8,128)(2,1)}, u32[]{:S(2)}) copy-start(bf16[26,2048]{1,0:T(8,128)(2,1)} %param.8) | copy-start | bytes 319492
  182.3 163.4 %copy-start.2 = (s32[256]{0:T(256)S(1)}, s32[256]{0:T(256)}, u32[]{:S(2)}) copy-start(s32[256]{0:T(256)} %param.11) | copy-start | bytes 3076
  182.4 229.9 %reduce-scatter.5.cloned.1.call-start = ((), (), s32[]{:S(2)}) async-start(), calls=%async_computation.4 | async-start | bytes 479232 | tf_op jit(solution)/shard_map/reduce_scatter | solution.py:47
Sparse Core Ops, SparseCore 0:
  9.7 54.6 all-gather.1
  182.5 163.2 reduce-scatter.2
  350.3 61.9 reduce-scatter.4
where the time goes:
time: 423 us; the launch traced here: 420 us
  waiting for transfers between devices  219 us (52%)
  local copies, waits for them, and re-layouts  116 us (27%)
  matrix products  46.1 us (11%)
  other arithmetic  25.3 us (6%)
  between operations  13.8 us (3%)
    reduce_scatter x1, waiting for transfers between devices, per_device(): lax.psum_scatter(terms.astype(jnp.bfloat16), 'row', scatter_dimension=0,...  160 us
    convert_element_type x2, local copies, waits for them, and re-layouts, dequantize(): values = unpack(packed).astype(jnp.float32)  72.9 us
    reduce_scatter x1, waiting for transfers between devices, per_device(): lax.psum_scatter(tenant_terms.astype(jnp.bfloat16), 'row', scatter_dimens...  57.5 us
    dot_general x1, matrix products, project(): lax.dot_general(panel_rows, weight, (((1,), (1,)), ((), ())), preferred_e...  39.6 us
    mul x2, local copies, waits for them, and re-layouts, dequantize(): values.reshape(n_groups, n_rows // n_groups, n_cols)  38 us
    another operation x1, other arithmetic, unpack(): stacked = jnp.stack([low_part - 8, high_part - 8], axis=-1)  14.3 us
    convert_element_type x1, other arithmetic, dequantize(): values = unpack(packed).astype(jnp.float32)  9.6 us
  transfers between devices with their start and end apart: 3, of which 2 were waited for; matrix products, arithmetic and copies ran while one was open for 34% of the time, Pallas kernels for 0%

commit v1 on v0

v1 whole, which is shorter than its diff:
```python
import functools

import jax
import jax.numpy as jnp
from jax import lax
from jax.experimental import pallas as pl
from jax.experimental.pallas import tpu as pltpu
from jax.sharding import PartitionSpec as P

TILE = 256
AHEAD = 5
F32 = jnp.float32
BF16 = jnp.bfloat16
PARTS = (32, 96)
GATHERS = (("a", 0, 0, 32), ("b", 1, 0, 32), ("c", 1, 32, 64))
CHUNKS = (
    (0, 32, True, "a", 0),
    (1, 32, True, "b", 0),
    (2, 32, False, "c", 0),
    (3, 32, True, "c", 32),
)
ORDER = ("a", "w", "b", "a", 0, "b", "c", 0, 1, 0, "c", 1, 2, 3, 0, 1, 3, 2, 1, 3, 2, 3, 2)


def place(x, y, z, core):
    x, y, z = x % 4, y % 4, z % 4
    return (y * 2 + z // 2) * 16 + x * 4 + (z % 2) * 2 + core


def route(move):
    return [
        (place(x, y, z, c), place(*move(x, y, z, c)))
        for x in range(4)
        for y in range(4)
        for z in range(4)
        for c in range(2)
    ]


def send(value, move):
    return lax.ppermute(value, ("row", "col"), route(move))


def y_up(x, y, z, c):
    return x, y + 1, z, c


def y_down(x, y, z, c):
    return x, y - 1, z, c


def z_across(x, y, z, c):
    return x, y, z + 2, c


def z_pair(x, y, z, c):
    return x, y, z + 1 - 2 * (z % 2), c


def x_up(x, y, z, c):
    return x + 1, y, z, c


def x_down(x, y, z, c):
    return x - 1, y, z, c


def x_across(x, y, z, c):
    return x + 2, y, z, c


def other_core(x, y, z, c):
    return x, y, z, 1 - c


def whole():
    return pl.BlockSpec(memory_space=pltpu.VMEM)


def anywhere():
    return pl.BlockSpec(memory_space=pl.ANY)


def chained(body, token, operands, in_specs, out_specs, out_shape, aliases=(), grid=(), scratch=(), mib=8, flops=1, name=""):
    n_in, n_out = len(in_specs), len(out_specs)

    def with_token(*refs):
        refs[n_in + 1 + n_out][...] = jnp.zeros((8, 128), F32)
        body(*refs[:n_in], *refs[n_in + 1 : n_in + 1 + n_out], *refs[n_in + 2 + n_out :])

    if grid:
        token_spec = pl.BlockSpec((8, 128), lambda i: (0, 0))
    else:
        token_spec = whole()
    *outs, token = pl.pallas_call(
        with_token,
        grid=grid,
        in_specs=[*in_specs, anywhere()],
        out_specs=[*out_specs, token_spec],
        out_shape=[*out_shape, jax.ShapeDtypeStruct((8, 128), F32)],
        scratch_shapes=scratch,
        input_output_aliases=dict(aliases),
        cost_estimate=pl.CostEstimate(flops=flops, bytes_accessed=1, transcendentals=0),
        compiler_params=pltpu.CompilerParams(vmem_limit_bytes=mib * 2**20),
        name=name,
    )(*operands, token)
    return outs, token


def split_body(x_ref, s_ref, s_out, *outs):
    into = lax.broadcasted_iota(jnp.int32, (256, 256), 0)
    col = lax.broadcasted_iota(jnp.int32, (256, 256), 1)
    pick = (into == jnp.where(col < 128, 2 * col, 2 * col - 255)).astype(BF16)
    for b in range(x_ref.shape[1] // 256):
        w = slice(256 * b, 256 * b + 256)
        x = jnp.dot(x_ref[:, w], pick, preferred_element_type=F32).astype(BF16)
        at = 0
        for out in outs:
            out[:, w] = x[at : at + out.shape[0]]
            at += out.shape[0]
        s_out[:, 0, w] = jnp.dot(s_ref[:, w], pick, preferred_element_type=F32)


def split_columns(x, scales, sizes):
    groups, k = scales.shape
    return chained(
        split_body,
        jnp.zeros((8, 128), F32),
        (x, scales),
        in_specs=[whole()] * 2,
        out_specs=[whole()] * (1 + len(sizes)),
        out_shape=[jax.ShapeDtypeStruct((groups, 1, k), F32)]
        + [jax.ShapeDtypeStruct((size, k), BF16) for size in sizes],
        name="split_columns",
    )


def join_body(rows, *refs):
    out, at = refs[-1], 0
    for (first, size), ref in zip(rows, refs):
        out[at : at + size] = ref[first : first + size]
        at += size


def join(token, *pieces):
    rows = tuple((first, size) for _, first, size in pieces)
    total, columns = sum(size for _, size in rows), pieces[0][0].shape[1]
    (out,), token = chained(
        functools.partial(join_body, rows),
        token,
        [array for array, _, _ in pieces],
        in_specs=[whole()] * len(pieces),
        out_specs=[whole()],
        out_shape=[jax.ShapeDtypeStruct((total, columns), BF16)],
        name="join",
    )
    return out, token


def dequantize_body(ahead, c_hbm, s_ref, w_hbm, c_v, w_v, c_sem, w_sem):
    tiles = c_hbm.shape[0]

    def fetch(i):
        at = lax.rem(i, ahead)
        return pltpu.make_async_copy(c_hbm.at[i], c_v.at[at], c_sem.at[at])

    def store(i):
        at = lax.rem(i, ahead)
        return pltpu.make_async_copy(w_v.at[at], w_hbm.at[i], w_sem.at[at])

    for i in range(ahead):
        fetch(i).start()

    def step(i, carry):
        at = lax.rem(i, ahead)
        fetch(i).wait()

        @pl.when(i >= ahead)
        def _():
            store(i - ahead).wait()

        for g in range(TILE // 128):
            rows = slice(128 * g, 128 * g + 128)
            for b in range(c_v.shape[2] // 128):
                q = c_v[at, rows, 128 * b : 128 * b + 128]
                scale = s_ref[TILE // 128 * i + g]
                for part, codes in enumerate((q & 15, q >> 4)):
                    cols = slice(256 * b + 128 * part, 256 * b + 128 * part + 128)
                    w = ((codes - 8).astype(F32) * scale[:, cols]).astype(BF16)
                    w_v[at, cols, rows] = w.T
        store(i).start()

        @pl.when(i + ahead < tiles)
        def _():
            fetch(i + ahead).start()

        return carry

    lax.fori_loop(0, tiles, step, 0)
    for i in range(tiles - ahead, tiles):
        store(i).wait()


def dequantize(token, codes, scales):
    ff, k = codes.shape
    tiles = ff // TILE
    (weight,), token = chained(
        functools.partial(dequantize_body, AHEAD),
        token,
        (codes.reshape(tiles, TILE, k), scales),
        in_specs=[anywhere(), whole()],
        out_specs=[anywhere()],
        out_shape=[jax.ShapeDtypeStruct((tiles, 2 * k, TILE), BF16)],
        scratch=[
            pltpu.VMEM((AHEAD, TILE, k), jnp.int32),
            pltpu.VMEM((AHEAD, 2 * k, TILE), BF16),
            pltpu.SemaphoreType.DMA((AHEAD,)),
            pltpu.SemaphoreType.DMA((AHEAD,)),
        ],
        mib=52,
        flops=11 * 10**9,
        name="dequantize",
    )
    return weight, token


def project_body(first, n, blocks, pieces, at_ref, mine, theirs, w_hbm, *refs):
    outs = refs[: len(pieces)]
    g_v, w_v, o_v, g_sem, w_sem, o_sem = refs[len(pieces) :]
    tiles, ring = w_hbm.shape[0], w_v.shape[0]
    ahead = 2

    def fetch(i):
        at = lax.rem(i, ring)
        return pltpu.make_async_copy(w_hbm.at[i], w_v.at[at], w_sem.at[at])

    def stores(i):
        at = pl.ds(pl.multiple_of(i * TILE, TILE), TILE)
        return [
            pltpu.make_async_copy(o_v.at[pl.ds(start, size), at], out.at[:, at], o_sem.at[p, i])
            for p, (out, (start, size)) in enumerate(zip(outs, pieces))
        ]

    y, z = lax.div(at_ref[0], 2), lax.rem(at_ref[0], 2)
    x, z_lo, core = lax.div(at_ref[1], 4), lax.rem(lax.div(at_ref[1], 2), 2), lax.rem(at_ref[1], 2)
    gathers = []
    for p, (dy, dz) in enumerate(blocks):
        to_y, to_z = lax.rem(y + dy, 4), lax.rem(z + dz, 2)
        block = lax.rem(to_y - x + 4, 4) * 2 + lax.rem(to_z + z_lo, 2)
        start = pl.multiple_of(block * (mine.shape[0] // 8) + first, 16)
        for other, source in enumerate((mine, theirs)):
            half = core if other == 0 else 1 - core
            at = pl.multiple_of((2 * p + half) * n, 16)
            gathers.append(
                pltpu.make_async_copy(
                    source.at[pl.ds(start, n), :],
                    g_v.at[pl.ds(at, n), :],
                    g_sem.at[2 * p + other],
                )
            )
    fetch(0).start()
    for copy in gathers:
        copy.start()
    fetch(1).start()
    for copy in gathers:
        copy.wait()

    def step(i, carry):
        fetch(i).wait()

        @pl.when(i + ahead < tiles)
        def _():
            fetch(i + ahead).start()

        at = pl.ds(pl.multiple_of(i * TILE, TILE), TILE)
        o_v[:, at] = jnp.dot(g_v[...], w_v[lax.rem(i, ring)], preferred_element_type=F32).astype(BF16)
        for copy in stores(i):
            copy.start()
        return carry

    lax.fori_loop(0, tiles, step, 0)

    def finish(i, carry):
        for copy in stores(i):
            copy.wait()
        return carry

    lax.fori_loop(0, tiles, finish, 0)


def project(token, here, mine, theirs, first, n, weight, blocks, pieces):
    tiles, k, _ = weight.shape
    ff = tiles * TILE
    return chained(
        functools.partial(project_body, first, n, blocks, pieces),
        token,
        (here, mine, theirs, weight),
        in_specs=[pl.BlockSpec(memory_space=pltpu.SMEM)] + [anywhere()] * 3,
        out_specs=[anywhere()] * len(pieces),
        out_shape=[jax.ShapeDtypeStruct((size, ff), BF16) for _, size in pieces],
        scratch=[
            pltpu.VMEM((16 * n, k), BF16),
            pltpu.VMEM((3, *weight.shape[1:]), BF16),
            pltpu.VMEM((16 * n, ff), BF16),
            pltpu.SemaphoreType.DMA((16,)),
            pltpu.SemaphoreType.DMA((3,)),
            pltpu.SemaphoreType.DMA((len(pieces), tiles)),
        ],
        mib=52,
        flops=4 * 16 * n * k * ff,
        name="project",
    )


STEPS = 2


def add_halves_body(up_ref, up_in, down_ref, down_in, up_out, down_out):
    up_out[...] = (up_ref[...].astype(F32) + up_in[...].astype(F32)).astype(BF16)
    down_out[...] = (down_ref[...].astype(F32) + down_in[...].astype(F32)).astype(BF16)


def add_halves(token, up, up_in, down, down_in):
    m, ff = up_in.shape
    low = pl.BlockSpec((m, ff // STEPS), lambda i: (0, i))
    high = pl.BlockSpec((m, ff // STEPS), lambda i: (1, i))
    return chained(
        add_halves_body,
        token,
        (up, up_in, down, down_in),
        grid=(STEPS,),
        in_specs=[low, low, high, low],
        out_specs=[low, high],
        out_shape=[jax.ShapeDtypeStruct(up.shape, BF16), jax.ShapeDtypeStruct(down.shape, BF16)],
        aliases={0: 0, 2: 1},
        name="add_halves",
    )


def sum_body(own_ref, up_ref, down_ref, keep_out, send_out):
    total = own_ref[...].astype(F32) + up_ref[...].astype(F32) + down_ref[...].astype(F32)
    m = keep_out.shape[0]
    keep_out[...] = total[:m]
    send_out[...] = total[m:].astype(BF16)


def sum_y(token, own, from_up, from_down):
    m2, ff = own.shape
    spec = pl.BlockSpec((m2, ff // STEPS), lambda i: (0, i))
    half = pl.BlockSpec((m2 // 2, ff // STEPS), lambda i: (0, i))
    return chained(
        sum_body,
        token,
        (own, from_up, from_down),
        grid=(STEPS,),
        in_specs=[spec] * 3,
        out_specs=[half] * 2,
        out_shape=[
            jax.ShapeDtypeStruct((m2 // 2, ff), F32),
            jax.ShapeDtypeStruct((m2 // 2, ff), BF16),
        ],
        name="sum_y",
    )


def sum_z_body(keep_ref, in_ref, *outs):
    at = 0
    for out in outs:
        rows = slice(at, at + out.shape[0])
        at += out.shape[0]
        out[...] = (keep_ref[rows].astype(F32) + in_ref[rows].astype(F32)).astype(out.dtype)


def sum_z(token, keep, arrived):
    m4, ff = keep.shape
    m = m4 // 4
    sizes = (m // 2, m // 2, m, m, m)
    spec = pl.BlockSpec((m4, ff // STEPS), lambda i: (0, i))
    return chained(
        sum_z_body,
        token,
        (keep, arrived),
        grid=(STEPS,),
        in_specs=[spec] * 2,
        out_specs=[pl.BlockSpec((size, ff // STEPS), lambda i: (0, i)) for size in sizes],
        out_shape=[jax.ShapeDtypeStruct((size, ff), BF16) for size in sizes],
        mib=12,
        name="sum_z",
    )


def finish_body(count, first, n, started, ids_ref, act_ref, l_ref, *refs):
    terms = refs[:count]
    out_ref, tenant_out = refs[-2:]
    gradient = terms[0][...].astype(F32)
    for term in terms[1:]:
        gradient = gradient + term[...].astype(F32)
    ids = jnp.concatenate([ids_ref[h : h + 1, first : first + n] for h in range(2)], axis=1)
    tenants = l_ref.shape[0]
    chosen = (ids == lax.broadcasted_iota(jnp.int32, (tenants, 2 * n), 0)).astype(BF16)
    gains = lax.dot_general(
        chosen, l_ref[...], (((0,), (0,)), ((), ())), preferred_element_type=F32
    )
    scaled = (gradient * gains).astype(BF16)
    total = None
    product = jnp.concatenate(
        [gradient[h * n : h * n + n] * act_ref[h].astype(F32) for h in range(2)], axis=0
    )
    coarse = product.astype(BF16)
    fine = (product - coarse.astype(F32)).astype(BF16)
    total = jnp.dot(chosen, coarse, preferred_element_type=F32) + jnp.dot(
        chosen, fine, preferred_element_type=F32
    )
    for h in range(2):
        out_ref[h] = scaled[h * n : h * n + n]
    if started:
        total = total + refs[count][...]
    tenant_out[...] = total.astype(tenant_out.dtype)


def finish(token, terms, first, n, ids, activations, l_ff, result, tenant_terms, last):
    tenants, ff = l_ff.shape
    wide = ff // STEPS
    started = tenant_terms is not None
    index = first // n
    rows = pl.BlockSpec((2, n, wide), lambda i: (0, index, i))
    flat = pl.BlockSpec((2 * n, wide), lambda i: (0, i))
    per_tenant = pl.BlockSpec((tenants, wide), lambda i: (0, i))
    operands = [ids, activations, l_ff, *terms]
    specs = [pl.BlockSpec(ids.shape, lambda i: (0, 0)), rows, per_tenant] + [flat] * len(terms)
    aliases = {}
    if started:
        if not last:
            aliases[len(operands)] = 1
        operands.append(tenant_terms)
        specs.append(per_tenant)
        aliases[len(operands)] = 0
        operands.append(result)
        specs.append(anywhere())
    return chained(
        functools.partial(finish_body, len(terms), first, n, started),
        token,
        operands,
        grid=(STEPS,),
        in_specs=specs,
        out_specs=[rows, per_tenant],
        out_shape=[
            jax.ShapeDtypeStruct(activations.shape, BF16),
            jax.ShapeDtypeStruct((tenants, ff), BF16 if last else F32),
        ],
        aliases=aliases,
        mib=14,
        name="finish",
    )


def gather_steps(part, paired, first, rows, kept):
    token = yield
    block, token = join(token, (part, first, rows), (paired, first, rows))
    token = yield token
    arrived = [send(block, move) for move in (x_down, x_across, x_up)]
    mine, token = join(token, *((array, 0, 2 * rows) for array in (block, *arrived)))
    kept.extend((mine, send(mine, other_core)))
    yield token


Y_BLOCKS = tuple((dy, dz) for dy in (2, 1, 3, 0) for dz in (0, 1))
Z_BLOCKS = tuple((dy, dz) for dz in (1, 0) for dy in (2, 1, 3, 0))


def chunk_steps(n, y_first, gathered, first, here, weights, tail):
    m = 2 * n
    token = yield
    if y_first:
        pieces = ((0, m), (m, m), (2 * m, 2 * m), (4 * m, 2 * m), (6 * m, 2 * m))
        (far_up, far_down, up, down, own), token = project(
            token, here, *gathered, first, n, *weights, Y_BLOCKS, pieces
        )
        token = yield token
        (up, down), token = add_halves(token, up, send(far_up, y_up), down, send(far_down, y_down))
        token = yield token
        (keep, leaves), token = sum_y(token, own, send(up, y_up), send(down, y_down))
        parts = (keep, send(leaves, z_across))
    else:
        pieces = ((0, 4 * m), (4 * m, 4 * m))
        (leaves, keep), token = project(
            token, here, *gathered, first, n, *weights, Z_BLOCKS, pieces
        )
        token = yield token
        (far_up, far_down, up, down, own), token = sum_z(token, keep, send(leaves, z_across))
        token = yield token
        (up, down), token = add_halves(token, up, send(far_up, y_up), down, send(far_down, y_down))
        parts = (own, send(up, y_up), send(down, y_down))
    token = yield token
    yield tail(token, parts)


def per_device(out_grad, codes, scales, activations, l_ff, tenant_ids):
    here = jnp.stack([lax.axis_index("row"), lax.axis_index("col")]).astype(jnp.int32)
    tokens, k = out_grad.shape
    ff = codes.shape[0]
    tenants = l_ff.shape[0]
    (split_scales, *parts), token = split_columns(out_grad, scales, PARTS)
    pairs = [(part, send(part, z_pair)) for part in parts]
    ids = tenant_ids.reshape(2, tokens)
    act = activations.reshape(2, tokens, ff)

    state = {"result": None, "terms": None}
    steps, kept, weights = {}, {}, []

    def weight_steps():
        token = yield
        weight, token = dequantize(token, codes, split_scales)
        weights.append(weight)
        yield token

    steps["w"] = weight_steps()
    for name, part, first, rows in GATHERS:
        kept[name] = []
        steps[name] = gather_steps(*pairs[part], first, rows, kept[name])
    first = 0
    for name, n, y_first, part, start in CHUNKS:

        def tail(token, terms, n=n, first=first, last=name == ORDER[-1]):
            (state["result"], state["terms"]), token = finish(
                token, terms, first, n, ids, act, l_ff, state["result"], state["terms"], last
            )
            return token

        steps[name] = chunk_steps(n, y_first, kept[part], start, here, weights, tail)
        first += n
    for generator in steps.values():
        next(generator)
    for name in ORDER:
        token = steps[name].send(token)
    n_row = lax.axis_size("row")
    terms, result = state["terms"], state["result"]
    arrived = lax.all_to_all(terms.reshape(n_row, tenants // n_row, ff), "row", 0, 0)
    tenant_grad = jnp.sum(arrived.astype(F32), axis=0)
    return result.reshape(2 * tokens, ff), tenant_grad


def solution(mesh):
    in_specs = (
        P("col", "row"),
        P("col", "row"),
        P("col", "row"),
        P("row", "col"),
        P(None, "col"),
        P("row"),
    )
    out_specs = (P("row", "col"), P("row", "col"))
    return jax.shard_map(
        per_device, mesh=mesh, in_specs=in_specs, out_specs=out_specs, check_vma=False
    )
```

time: 423 us -> 198 us (0.47)
  waiting for transfers between devices: 219 us -> 46.6 us
  local copies, waits for them, and re-layouts: 116 us -> 4.32 us
  Pallas kernels: 0 us -> 78.2 us
  starting transfers between devices: 0.3 us -> 53.1 us
  matrix products: 46.1 us -> 0 us
  other arithmetic: 25.3 us -> 0.77 us
  blocking collectives: 0 us -> 13.5 us
  between operations: 13.8 us -> 1.01 us
    reduce_scatter x2 -> x0, waiting for transfers between devices: 218 us -> none  [the longest x1 160 us: per_device(): lax.psum_scatter(terms.astype(jnp.bfloat16), 'row', scatter_dimension=0,...]
    pallas_call x0 -> x24, Pallas kernels: none -> 78.2 us  [chained(): pl.pallas_call(with_token, grid=grid, in_specs=[*in_specs, anywhere()], o...]
    convert_element_type x2 -> x0, local copies, waits for them, and re-layouts: 72.9 us -> none  [dequantize(): values = unpack(packed).astype(jnp.float32)]
    ppermute x0 -> x34, starting transfers between devices: none -> 53.1 us  [send(): return lax.ppermute(value, ('row', 'col'), route(move))]
    ppermute x0 -> x34, waiting for transfers between devices: none -> 46.6 us  [send(): return lax.ppermute(value, ('row', 'col'), route(move))]
    dot_general x3 -> x0, matrix products: 46.1 us -> none  [the longest x1 39.6 us: project(): lax.dot_general(panel_rows, weight, (((1,), (1,)), ((), ())), preferred_e...]
    mul x2 -> x0, local copies, waits for them, and re-layouts: 38 us -> none  [dequantize(): values.reshape(n_groups, n_rows // n_groups, n_cols)]
    another operation x1, other arithmetic: 14.3 us -> 0.08 us  [per_device(): jnp.stack([lax.axis_index('row'), lax.axis_index('col')]).astype(jnp.int32)]
  transfers between devices with their start and end apart: 3 -> 34, of which waited for: 2 -> 10; matrix products, arithmetic and copies ran while one was open for 34% -> 0% of each run, Pallas kernels for 0% -> 38%
where the time goes in v1:
time: 198 us; the launch traced here: 197 us
  Pallas kernels  78.2 us (39%)
  starting transfers between devices  53.1 us (27%)
  waiting for transfers between devices  46.6 us (24%)
  blocking collectives  13.5 us (7%)
  local copies, waits for them, and re-layouts  4.32 us (2%)
    pallas_call x24, Pallas kernels, chained(): pl.pallas_call(with_token, grid=grid, in_specs=[*in_specs, anywhere()], o...  78.2 us
    ppermute x34, starting transfers between devices, send(): return lax.ppermute(value, ('row', 'col'), route(move))  53.1 us
    ppermute x34, waiting for transfers between devices, send(): return lax.ppermute(value, ('row', 'col'), route(move))  46.6 us
    all_to_all x1, blocking collectives, per_device(): lax.all_to_all(terms.reshape(n_row, tenants // n_row, ff), 'row', 0, 0)  13.5 us
    unnamed x36, local copies, waits for them, and re-layouts  4.32 us
  transfers between devices with their start and end apart: 34, of which 10 were waited for; matrix products, arithmetic and copies ran while one was open for 0% of the time, Pallas kernels for 38%

profile of v1, /device:TPU:0, one launch (start us, length us, event | category | flops | bytes accessed | tf_op | source)
XLA Modules:
  0.0 197.5 jit_solution(5120755979714232648)
XLA Ops:
  3.0 2.1 %collective-permute-start.1 = (bf16[32,2048]{1,0:T(8,128)(2,1)S(1)}, bf16[32,2048]{1,0:T(8,128)(2,1)S(1)}, u32[]{:S(2)}, u32[]{:S(2)}) collective-permute-start(bf16[32,2048]{1,0:T(8,128)(2,1)S(1)} %get-tuple-element.81.refs_0_), channel_id=1, source_target_pairs={{0,2},{1,3},{2,0},{3,1},{16,18},{17,19},{18,16},{19,17},{32,34},{3... | collective-permute-start | bytes 393224 | tf_op jit(solution)/shard_map/ppermute | solution.py:41
  5.2 4.3 %collective-permute-done.1.refs_1_ = bf16[32,2048]{1,0:T(8,128)(2,1)S(1)} collective-permute-done((bf16[32,2048]{1,0:T(8,128)(2,1)S(1)}, bf16[32,2048]{1,0:T(8,128)(2,1)S(1)}, u32[]{:S(2)}, u32[]{:S(2)}) %collective-permute-start.1) | collective-permute-done | bytes 131104 | tf_op jit(solution)/shard_map/ppermute | solution.py:41
  11.1 2.7 %collective-permute-start.6 = (bf16[64,2048]{1,0:T(8,128)(2,1)S(1)}, bf16[64,2048]{1,0:T(8,128)(2,1)S(1)}, u32[]{:S(2)}, u32[]{:S(2)}) collective-permute-start(bf16[64,2048]{1,0:T(8,128)(2,1)S(1)} %get-tuple-element.86.refs_0_), channel_id=1, source_target_pairs={{0,8},{1,9},{2,10},{3,11},{16,24},{17,25},{18,26},{19,27},{32,40},... | collective-permute-start | bytes 786440 | tf_op jit(solution)/shard_map/ppermute | solution.py:41
  15.3 10.6 %dequantize.1 = (bf16[13,2048,256]{2,1,0:T(8,128)(2,1)}, f32[8,128]{1,0:T(8,128)S(1)}) custom-call(s32[13,256,1024]{2,1,0:T(8,128)} %bitcast.17, f32[26,1,2048]{2,1,0:T(1,128)S(1)} %get-tuple-element.80.refs_1_, f32[8,128]{1,0:T(8,128)S(1)} %get-tuple-element.83.refs_2_), custom_call_target="tpu_custom_call" | custom-call | flops 11000000512 | bytes 1 | tf_op jit(solution)/shard_map/dequantize/pallas_call | solution.py:95
  30.6 13.7 %project.4 = (bf16[64,3328]{1,0:T(8,128)(2,1)S(1)}, bf16[64,3328]{1,0:T(8,128)(2,1)S(1)}, bf16[128,3328]{1,0:T(8,128)(2,1)S(1)}, bf16[128,3328]{1,0:T(8,128)(2,1...) custom-call(s32[2]{0:T(128)S(1)} %pad_add_fusion.refs_0_, bf16[256,2048]{1,0:T(8,128)(2,1)} %copy-done.14, ...), custom_call_target="tpu_custom_call" | custom-call | flops 13958643712 | bytes 1 | tf_op jit(solution)/shard_map/project/pallas_call | solution.py:95
  46.2 1.7 collective-permute-start.13
  48.7 2.2 %collective-permute-start.10 = (bf16[128,2048]{1,0:T(8,128)(2,1)S(1)}, bf16[128,2048]{1,0:T(8,128)(2,1)S(1)}, u32[]{:S(2)}, u32[]{:S(2)}) collective-permute-start(bf16[128,2048]{1,0:T(8,128)(2,1)S(1)} %get-tuple-element.93.refs_0_), channel_id=1, source_target_pairs={{0,8},{1,9},{2,10},{3,11},{16,24},{17,25},{18,26},{19,27},{32,40},... | collective-permute-start | bytes 1572872 | tf_op jit(solution)/shard_map/ppermute | solution.py:41
  50.9 7.2 %collective-permute-done.12.refs_1_ = bf16[64,3328]{1,0:T(8,128)(2,1)S(1)} collective-permute-done((bf16[64,3328]{1,0:T(8,128)(2,1)S(1)}, bf16[64,3328]{1,0:T(8,128)(2,1)S(1)}, u32[]{:S(2)}, u32[]{:S(2)}) %collective-permute-start.12) | collective-permute-done | bytes 426016 | tf_op jit(solution)/shard_map/ppermute | solution.py:41
  60.3 2.9 %collective-permute-start.15 = (bf16[128,3328]{1,0:T(8,128)(2,1)S(1)}, bf16[128,3328]{1,0:T(8,128)(2,1)S(1)}, u32[]{:S(2)}, u32[]{:S(2)}) collective-permute-start(bf16[128,3328]{1,0:T(8,128)(2,1)S(1)} %get-tuple-element.101), channel_id=1, source_target_pairs={{0,96},{1,97},{2,98},{3,99},{16,112},{17,113},{18,114},{19,115},{3... | collective-permute-start | bytes 2555912 | tf_op jit(solution)/shard_map/ppermute | solution.py:41
  63.2 13.8 %project.5 = (bf16[64,3328]{1,0:T(8,128)(2,1)S(1)}, bf16[64,3328]{1,0:T(8,128)(2,1)S(1)}, bf16[128,3328]{1,0:T(8,128)(2,1)S(1)}, bf16[128,3328]{1,0:T(8,128)(2,1...) custom-call(s32[2]{0:T(128)S(1)} %pad_add_fusion.refs_0_, bf16[256,2048]{1,0:T(8,128)(2,1)} %copy-done.13, ...), custom_call_target="tpu_custom_call" | custom-call | flops 13958643712 | bytes 1 | tf_op jit(solution)/shard_map/project/pallas_call | solution.py:95
  77.0 4.5 %collective-permute-done.14.refs_1_ = bf16[128,3328]{1,0:T(8,128)(2,1)S(1)} collective-permute-done((bf16[128,3328]{1,0:T(8,128)(2,1)S(1)}, bf16[128,3328]{1,0:T(8,128)(2,1)S(1)}, u32[]{:S(2)}, u32[]{:S(2)}) %collective-permute-start.14) | collective-permute-done | bytes 852000 | tf_op jit(solution)/shard_map/ppermute | solution.py:41
  83.4 2.9 %collective-permute-start.19 = (bf16[64,3328]{1,0:T(8,128)(2,1)S(1)}, bf16[64,3328]{1,0:T(8,128)(2,1)S(1)}, u32[]{:S(2)}, u32[]{:S(2)}) collective-permute-start(bf16[64,3328]{1,0:T(8,128)(2,1)S(1)} %get-tuple-element.110), channel_id=1, source_target_pairs={{0,96},{1,97},{2,98},{3,99},{16,112},{17,113},{18,114},{19,115},{3... | collective-permute-start | bytes 1277960 | tf_op jit(solution)/shard_map/ppermute | solution.py:41
  86.3 3.9 %collective-permute-start.25 = (bf16[64,3328]{1,0:T(8,128)(2,1)}, bf16[64,3328]{1,0:T(8,128)(2,1)S(1)}, u32[]{:S(2)}, u32[]{:S(2)}) collective-permute-start(bf16[64,3328]{1,0:T(8,128)(2,1)} %get-tuple-element.124), channel_id=1, source_target_pairs={{0,16},{1,17},{2,18},{3,19},{16,0},{17,1},{18,2},{19,3},{32,48},{3... | collective-permute-start | bytes 1277960 | tf_op jit(solution)/shard_map/ppermute | solution.py:41
  90.2 6.2 %collective-permute-done.18.refs_1_ = bf16[64,3328]{1,0:T(8,128)(2,1)S(1)} collective-permute-done((bf16[64,3328]{1,0:T(8,128)(2,1)S(1)}, bf16[64,3328]{1,0:T(8,128)(2,1)S(1)}, u32[]{:S(2)}, u32[]{:S(2)}) %collective-permute-start.18) | collective-permute-done | bytes 426016 | tf_op jit(solution)/shard_map/ppermute | solution.py:41
  98.1 2.1 %collective-permute-start.24 = (bf16[128,3328]{1,0:T(8,128)(2,1)S(1)}, bf16[128,3328]{1,0:T(8,128)(2,1)S(1)}, u32[]{:S(2)}, u32[]{:S(2)}) collective-permute-start(bf16[128,3328]{1,0:T(8,128)(2,1)S(1)} %get-tuple-element.122), channel_id=1, source_target_pairs={{0,96},{1,97},{2,98},{3,99},{16,112},{17,113},{18,114},{19,115},{3... | collective-permute-start | bytes 2555912 | tf_op jit(solution)/shard_map/ppermute | solution.py:41
  101.5 13.1 %project.6 = (bf16[256,3328]{1,0:T(8,128)(2,1)}, bf16[256,3328]{1,0:T(8,128)(2,1)}, f32[8,128]{1,0:T(8,128)S(1)}) custom-call(s32[2]{0:T(128)S(1)} %pad_add_fusion.refs_0_, bf16[512,2048]{1,0:T(8,128)(2,1)} %copy-done.12, bf16[512,2048]{1,0:T(8,128)(2,1)} %copy-done.15, bf16[13,2048,256]{2,1,0:T(8,128)(2,1)} %get-tuple-element.89.refs_3_, ...), custom_call_target="tpu_custom_call" | custom-call | flops 13958643712 | bytes 1 | tf_op jit(solution)/shard_map/project/pallas_call | solution.py:95
  114.6 4.0 %collective-permute-start.20 = (bf16[256,3328]{1,0:T(8,128)(2,1)}, bf16[256,3328]{1,0:T(8,128)(2,1)S(1)}, u32[]{:S(2)}, u32[]{:S(2)}) collective-permute-start(bf16[256,3328]{1,0:T(8,128)(2,1)} %get-tuple-element.114), channel_id=1, source_target_pairs={{0,16},{1,17},{2,18},{3,19},{16,0},{17,1},{18,2},{19,3},{32,48},{3... | collective-permute-start | bytes 5111816 | tf_op jit(solution)/shard_map/ppermute | solution.py:41
  118.6 13.8 %project.7 = (bf16[64,3328]{1,0:T(8,128)(2,1)S(1)}, bf16[64,3328]{1,0:T(8,128)(2,1)S(1)}, bf16[128,3328]{1,0:T(8,128)(2,1)S(1)}, bf16[128,3328]{1,0:T(8,128)(2,1...) custom-call(s32[2]{0:T(128)S(1)} %pad_add_fusion.refs_0_, bf16[512,2048]{1,0:T(8,128)(2,1)} %copy-done.12, ...), custom_call_target="tpu_custom_call" | custom-call | flops 13958643712 | bytes 1 | tf_op jit(solution)/shard_map/project/pallas_call | solution.py:95
  132.6 3.2 %collective-permute-start.22 = (bf16[64,3328]{1,0:T(8,128)(2,1)S(1)}, bf16[64,3328]{1,0:T(8,128)(2,1)S(1)}, u32[]{:S(2)}, u32[]{:S(2)}) collective-permute-start(bf16[64,3328]{1,0:T(8,128)(2,1)S(1)} %get-tuple-element.119), channel_id=1, source_target_pairs={{0,96},{1,97},{2,98},{3,99},{16,112},{17,113},{18,114},{19,115},{3... | collective-permute-start | bytes 1277960 | tf_op jit(solution)/shard_map/ppermute | solution.py:41
  135.8 1.8 finish.4
  138.3 6.0 %collective-permute-done.21.refs_1_ = bf16[64,3328]{1,0:T(8,128)(2,1)S(1)} collective-permute-done((bf16[64,3328]{1,0:T(8,128)(2,1)S(1)}, bf16[64,3328]{1,0:T(8,128)(2,1)S(1)}, u32[]{:S(2)}, u32[]{:S(2)}) %collective-permute-start.21) | collective-permute-done | bytes 426016 | tf_op jit(solution)/shard_map/ppermute | solution.py:41
  144.8 3.2 %collective-permute-start.29 = (bf16[128,3328]{1,0:T(8,128)(2,1)S(1)}, bf16[128,3328]{1,0:T(8,128)(2,1)S(1)}, u32[]{:S(2)}, u32[]{:S(2)}) collective-permute-start(bf16[128,3328]{1,0:T(8,128)(2,1)S(1)} %get-tuple-element.136), channel_id=1, source_target_pairs={{0,96},{1,97},{2,98},{3,99},{16,112},{17,113},{18,114},{19,115},{3... | collective-permute-start | bytes 2555912 | tf_op jit(solution)/shard_map/ppermute | solution.py:41
  148.4 8.6 %collective-permute-done.20.refs_1_ = bf16[256,3328]{1,0:T(8,128)(2,1)S(1)} collective-permute-done((bf16[256,3328]{1,0:T(8,128)(2,1)}, bf16[256,3328]{1,0:T(8,128)(2,1)S(1)}, u32[]{:S(2)}, u32[]{:S(2)}) %collective-permute-start.20) | collective-permute-done | bytes 1703968 | tf_op jit(solution)/shard_map/ppermute | solution.py:41
  157.9 3.2 %collective-permute-start.27 = (bf16[32,3328]{1,0:T(8,128)(2,1)S(1)}, bf16[32,3328]{1,0:T(8,128)(2,1)S(1)}, u32[]{:S(2)}, u32[]{:S(2)}) collective-permute-start(bf16[32,3328]{1,0:T(8,128)(2,1)S(1)} %get-tuple-element.133), channel_id=1, source_target_pairs={{0,96},{1,97},{2,98},{3,99},{16,112},{17,113},{18,114},{19,115},{3... | collective-permute-start | bytes 638984 | tf_op jit(solution)/shard_map/ppermute | solution.py:41
  161.1 3.3 %collective-permute-done.30.refs_4_ = bf16[64,3328]{1,0:T(8,128)(2,1)S(1)} collective-permute-done((bf16[64,3328]{1,0:T(8,128)(2,1)S(1)}, bf16[64,3328]{1,0:T(8,128)(2,1)S(1)}, u32[]{:S(2)}, u32[]{:S(2)}) %collective-permute-start.30) | collective-permute-done | bytes 426016 | tf_op jit(solution)/shard_map/ppermute | solution.py:41
  164.4 1.9 finish.5
  167.7 2.6 %collective-permute-start.33 = (bf16[64,3328]{1,0:T(8,128)(2,1)S(1)}, bf16[64,3328]{1,0:T(8,128)(2,1)S(1)}, u32[]{:S(2)}, u32[]{:S(2)}) collective-permute-start(bf16[64,3328]{1,0:T(8,128)(2,1)S(1)} %get-tuple-element.147), channel_id=1, source_target_pairs={{0,16},{1,17},{2,18},{3,19},{16,0},{17,1},{18,2},{19,3},{32,48},{3... | collective-permute-start | bytes 1277960 | tf_op jit(solution)/shard_map/ppermute | solution.py:41
  170.6 3.2 %collective-permute-start.32 = (bf16[64,3328]{1,0:T(8,128)(2,1)S(1)}, bf16[64,3328]{1,0:T(8,128)(2,1)S(1)}, u32[]{:S(2)}, u32[]{:S(2)}) collective-permute-start(bf16[64,3328]{1,0:T(8,128)(2,1)S(1)} %get-tuple-element.145), channel_id=1, source_target_pairs={{0,96},{1,97},{2,98},{3,99},{16,112},{17,113},{18,114},{19,115},{3... | collective-permute-start | bytes 1277960 | tf_op jit(solution)/shard_map/ppermute | solution.py:41
  173.8 4.8 %collective-permute-done.33.refs_4_ = bf16[64,3328]{1,0:T(8,128)(2,1)S(1)} collective-permute-done((bf16[64,3328]{1,0:T(8,128)(2,1)S(1)}, bf16[64,3328]{1,0:T(8,128)(2,1)S(1)}, u32[]{:S(2)}, u32[]{:S(2)}) %collective-permute-start.33) | collective-permute-done | bytes 426016 | tf_op jit(solution)/shard_map/ppermute | solution.py:41
  178.7 1.9 finish.6
  181.4 1.9 finish.7
  183.3 13.5 %all_to_all.5 = bf16[8,8,3328]{2,1,0:T(8,128)(2,1)S(1)} all-to-all(bf16[8,8,3328]{2,1,0:T(8,128)(2,1)S(1)} %bitcast.11), channel_id=1, replica_groups=mesh['row'=8,'col'=16] {'row'}, dimensions={0} | all-to-all | bytes 851968 | tf_op jit(solution)/shard_map/all_to_all | solution.py:538
  (100 shorter events, 25.8 us)
Async XLA Ops:
  5.1 20.8 %collective-permute-start = (bf16[96,2048]{1,0:T(8,128)(2,1)S(1)}, bf16[96,2048]{1,0:T(8,128)(2,1)S(1)}, u32[]{:S(2)}, u32[]{:S(2)}) collective-permute-start(bf16[96,2048]{1,0:T(8,128)(2,1)S(1)} %get-tuple-element.79.refs_0_), channel_id=1, source_target_pairs={{0,2},{1,3},{2,0},{3,1},{16,18},{17,19},{18,16},{19,17},{32,34},{3... | collective-permute-start | bytes 1179656 | tf_op jit(solution)/shard_map/ppermute | solution.py:41
  9.5 16.5 %collective-permute-start.7 = (bf16[64,2048]{1,0:T(8,128)(2,1)S(1)}, bf16[64,2048]{1,0:T(8,128)(2,1)S(1)}, u32[]{:S(2)}, u32[]{:S(2)}) collective-permute-start(bf16[64,2048]{1,0:T(8,128)(2,1)S(1)} %get-tuple-element.86.refs_0_), channel_id=1, source_target_pairs={{0,4},{1,5},{2,6},{3,7},{16,20},{17,21},{18,22},{19,23},{32,36},{3... | collective-permute-start | bytes 786440 | tf_op jit(solution)/shard_map/ppermute | solution.py:41
  11.1 14.8 %collective-permute-start.6 = (bf16[64,2048]{1,0:T(8,128)(2,1)S(1)}, bf16[64,2048]{1,0:T(8,128)(2,1)S(1)}, u32[]{:S(2)}, u32[]{:S(2)}) collective-permute-start(bf16[64,2048]{1,0:T(8,128)(2,1)S(1)} %get-tuple-element.86.refs_0_), channel_id=1, source_target_pairs={{0,8},{1,9},{2,10},{3,11},{16,24},{17,25},{18,26},{19,27},{32,40},... | collective-permute-start | bytes 786440 | tf_op jit(solution)/shard_map/ppermute | solution.py:41
  13.9 12.1 %collective-permute-start.5 = (bf16[64,2048]{1,0:T(8,128)(2,1)S(1)}, bf16[64,2048]{1,0:T(8,128)(2,1)S(1)}, u32[]{:S(2)}, u32[]{:S(2)}) collective-permute-start(bf16[64,2048]{1,0:T(8,128)(2,1)S(1)} %get-tuple-element.86.refs_0_), channel_id=1, source_target_pairs={{0,12},{1,13},{2,14},{3,15},{16,28},{17,29},{18,30},{19,31},{32,44... | collective-permute-start | bytes 786440 | tf_op jit(solution)/shard_map/ppermute | solution.py:41
  26.2 18.1 %collective-permute-start.4 = (bf16[64,2048]{1,0:T(8,128)(2,1)S(1)}, bf16[64,2048]{1,0:T(8,128)(2,1)S(1)}, u32[]{:S(2)}, u32[]{:S(2)}) collective-permute-start(bf16[64,2048]{1,0:T(8,128)(2,1)S(1)} %get-tuple-element.85.refs_0_), channel_id=1, source_target_pairs={{0,4},{1,5},{2,6},{3,7},{16,20},{17,21},{18,22},{19,23},{32,36},{3... | collective-permute-start | bytes 786440 | tf_op jit(solution)/shard_map/ppermute | solution.py:41
  26.9 17.5 %collective-permute-start.3 = (bf16[64,2048]{1,0:T(8,128)(2,1)S(1)}, bf16[64,2048]{1,0:T(8,128)(2,1)S(1)}, u32[]{:S(2)}, u32[]{:S(2)}) collective-permute-start(bf16[64,2048]{1,0:T(8,128)(2,1)S(1)} %get-tuple-element.85.refs_0_), channel_id=1, source_target_pairs={{0,8},{1,9},{2,10},{3,11},{16,24},{17,25},{18,26},{19,27},{32,40},... | collective-permute-start | bytes 786440 | tf_op jit(solution)/shard_map/ppermute | solution.py:41
  28.0 16.4 %collective-permute-start.2 = (bf16[64,2048]{1,0:T(8,128)(2,1)S(1)}, bf16[64,2048]{1,0:T(8,128)(2,1)S(1)}, u32[]{:S(2)}, u32[]{:S(2)}) collective-permute-start(bf16[64,2048]{1,0:T(8,128)(2,1)S(1)} %get-tuple-element.85.refs_0_), channel_id=1, source_target_pairs={{0,12},{1,13},{2,14},{3,15},{16,28},{17,29},{18,30},{19,31},{32,44... | collective-permute-start | bytes 786440 | tf_op jit(solution)/shard_map/ppermute | solution.py:41
  44.5 15.8 %collective-permute-start.16 = (bf16[256,2048]{1,0:T(8,128)(2,1)S(1)}, bf16[256,2048]{1,0:T(8,128)(2,1)S(1)}, u32[]{:S(2)}, u32[]{:S(2)}) collective-permute-start(bf16[256,2048]{1,0:T(8,128)(2,1)S(1)} %get-tuple-element.102.refs_1_), channel_id=1, source_target_pairs={{0,1},{1,0},{2,3},{3,2},{16,17},{17,16},{18,19},{19,18},{32,33},{3... | collective-permute-start | bytes 3145736 | tf_op jit(solution)/shard_map/ppermute | solution.py:41
  44.6 13.5 %collective-permute-start.12 = (bf16[64,3328]{1,0:T(8,128)(2,1)S(1)}, bf16[64,3328]{1,0:T(8,128)(2,1)S(1)}, u32[]{:S(2)}, u32[]{:S(2)}) collective-permute-start(bf16[64,3328]{1,0:T(8,128)(2,1)S(1)} %get-tuple-element.96), channel_id=1, source_target_pairs={{0,32},{1,33},{2,34},{3,35},{16,48},{17,49},{18,50},{19,51},{32,64... | collective-permute-start | bytes 1277960 | tf_op jit(solution)/shard_map/ppermute | solution.py:41
  46.2 13.2 %collective-permute-start.13 = (bf16[64,3328]{1,0:T(8,128)(2,1)S(1)}, bf16[64,3328]{1,0:T(8,128)(2,1)S(1)}, u32[]{:S(2)}, u32[]{:S(2)}) collective-permute-start(bf16[64,3328]{1,0:T(8,128)(2,1)S(1)} %get-tuple-element.98), channel_id=1, source_target_pairs={{0,96},{1,97},{2,98},{3,99},{16,112},{17,113},{18,114},{19,115},{3... | collective-permute-start | bytes 1277960 | tf_op jit(solution)/shard_map/ppermute | solution.py:41
  47.9 34.8 %collective-permute-start.11 = (bf16[128,2048]{1,0:T(8,128)(2,1)S(1)}, bf16[128,2048]{1,0:T(8,128)(2,1)S(1)}, u32[]{:S(2)}, u32[]{:S(2)}) collective-permute-start(bf16[128,2048]{1,0:T(8,128)(2,1)S(1)} %get-tuple-element.93.refs_0_), channel_id=1, source_target_pairs={{0,4},{1,5},{2,6},{3,7},{16,20},{17,21},{18,22},{19,23},{32,36},{3... | collective-permute-start | bytes 1572872 | tf_op jit(solution)/shard_map/ppermute | solution.py:41
  48.7 34.0 %collective-permute-start.10 = (bf16[128,2048]{1,0:T(8,128)(2,1)S(1)}, bf16[128,2048]{1,0:T(8,128)(2,1)S(1)}, u32[]{:S(2)}, u32[]{:S(2)}) collective-permute-start(bf16[128,2048]{1,0:T(8,128)(2,1)S(1)} %get-tuple-element.93.refs_0_), channel_id=1, source_target_pairs={{0,8},{1,9},{2,10},{3,11},{16,24},{17,25},{18,26},{19,27},{32,40},... | collective-permute-start | bytes 1572872 | tf_op jit(solution)/shard_map/ppermute | solution.py:41
  58.1 24.6 %collective-permute-start.9 = (bf16[128,2048]{1,0:T(8,128)(2,1)S(1)}, bf16[128,2048]{1,0:T(8,128)(2,1)S(1)}, u32[]{:S(2)}, u32[]{:S(2)}) collective-permute-start(bf16[128,2048]{1,0:T(8,128)(2,1)S(1)} %get-tuple-element.93.refs_0_), channel_id=1, source_target_pairs={{0,12},{1,13},{2,14},{3,15},{16,28},{17,29},{18,30},{19,31},{32,44... | collective-permute-start | bytes 1572872 | tf_op jit(solution)/shard_map/ppermute | solution.py:41
  59.9 21.6 %collective-permute-start.14 = (bf16[128,3328]{1,0:T(8,128)(2,1)S(1)}, bf16[128,3328]{1,0:T(8,128)(2,1)S(1)}, u32[]{:S(2)}, u32[]{:S(2)}) collective-permute-start(bf16[128,3328]{1,0:T(8,128)(2,1)S(1)} %get-tuple-element.100), channel_id=1, source_target_pairs={{0,32},{1,33},{2,34},{3,35},{16,48},{17,49},{18,50},{19,51},{32,64... | collective-permute-start | bytes 2555912 | tf_op jit(solution)/shard_map/ppermute | solution.py:41
  60.3 21.2 %collective-permute-start.15 = (bf16[128,3328]{1,0:T(8,128)(2,1)S(1)}, bf16[128,3328]{1,0:T(8,128)(2,1)S(1)}, u32[]{:S(2)}, u32[]{:S(2)}) collective-permute-start(bf16[128,3328]{1,0:T(8,128)(2,1)S(1)} %get-tuple-element.101), channel_id=1, source_target_pairs={{0,96},{1,97},{2,98},{3,99},{16,112},{17,113},{18,114},{19,115},{3... | collective-permute-start | bytes 2555912 | tf_op jit(solution)/shard_map/ppermute | solution.py:41
  82.9 17.3 %collective-permute-start.17 = (bf16[512,2048]{1,0:T(8,128)(2,1)S(1)}, bf16[512,2048]{1,0:T(8,128)(2,1)S(1)}, u32[]{:S(2)}, u32[]{:S(2)}) collective-permute-start(bf16[512,2048]{1,0:T(8,128)(2,1)S(1)} %get-tuple-element.106.refs_1_), channel_id=1, source_target_pairs={{0,1},{1,0},{2,3},{3,2},{16,17},{17,16},{18,19},{19,18},{32,33},{3... | collective-permute-start | bytes 6291464 | tf_op jit(solution)/shard_map/ppermute | solution.py:41
  83.0 13.4 %collective-permute-start.18 = (bf16[64,3328]{1,0:T(8,128)(2,1)S(1)}, bf16[64,3328]{1,0:T(8,128)(2,1)S(1)}, u32[]{:S(2)}, u32[]{:S(2)}) collective-permute-start(bf16[64,3328]{1,0:T(8,128)(2,1)S(1)} %get-tuple-element.108), channel_id=1, source_target_pairs={{0,32},{1,33},{2,34},{3,35},{16,48},{17,49},{18,50},{19,51},{32,64... | collective-permute-start | bytes 1277960 | tf_op jit(solution)/shard_map/ppermute | solution.py:41
  83.4 13.0 %collective-permute-start.19 = (bf16[64,3328]{1,0:T(8,128)(2,1)S(1)}, bf16[64,3328]{1,0:T(8,128)(2,1)S(1)}, u32[]{:S(2)}, u32[]{:S(2)}) collective-permute-start(bf16[64,3328]{1,0:T(8,128)(2,1)S(1)} %get-tuple-element.110), channel_id=1, source_target_pairs={{0,96},{1,97},{2,98},{3,99},{16,112},{17,113},{18,114},{19,115},{3... | collective-permute-start | bytes 1277960 | tf_op jit(solution)/shard_map/ppermute | solution.py:41
  86.3 46.3 %collective-permute-start.25 = (bf16[64,3328]{1,0:T(8,128)(2,1)}, bf16[64,3328]{1,0:T(8,128)(2,1)S(1)}, u32[]{:S(2)}, u32[]{:S(2)}) collective-permute-start(bf16[64,3328]{1,0:T(8,128)(2,1)} %get-tuple-element.124), channel_id=1, source_target_pairs={{0,16},{1,17},{2,18},{3,19},{16,0},{17,1},{18,2},{19,3},{32,48},{3... | collective-permute-start | bytes 1277960 | tf_op jit(solution)/shard_map/ppermute | solution.py:41
  96.9 40.7 %collective-permute-start.23 = (bf16[128,3328]{1,0:T(8,128)(2,1)S(1)}, bf16[128,3328]{1,0:T(8,128)(2,1)S(1)}, u32[]{:S(2)}, u32[]{:S(2)}) collective-permute-start(bf16[128,3328]{1,0:T(8,128)(2,1)S(1)} %get-tuple-element.121), channel_id=1, source_target_pairs={{0,32},{1,33},{2,34},{3,35},{16,48},{17,49},{18,50},{19,51},{32,64... | collective-permute-start | bytes 2555912 | tf_op jit(solution)/shard_map/ppermute | solution.py:41
  98.1 39.5 %collective-permute-start.24 = (bf16[128,3328]{1,0:T(8,128)(2,1)S(1)}, bf16[128,3328]{1,0:T(8,128)(2,1)S(1)}, u32[]{:S(2)}, u32[]{:S(2)}) collective-permute-start(bf16[128,3328]{1,0:T(8,128)(2,1)S(1)} %get-tuple-element.122), channel_id=1, source_target_pairs={{0,96},{1,97},{2,98},{3,99},{16,112},{17,113},{18,114},{19,115},{3... | collective-permute-start | bytes 2555912 | tf_op jit(solution)/shard_map/ppermute | solution.py:41
  114.6 42.3 %collective-permute-start.20 = (bf16[256,3328]{1,0:T(8,128)(2,1)}, bf16[256,3328]{1,0:T(8,128)(2,1)S(1)}, u32[]{:S(2)}, u32[]{:S(2)}) collective-permute-start(bf16[256,3328]{1,0:T(8,128)(2,1)} %get-tuple-element.114), channel_id=1, source_target_pairs={{0,16},{1,17},{2,18},{3,19},{16,0},{17,1},{18,2},{19,3},{32,48},{3... | collective-permute-start | bytes 5111816 | tf_op jit(solution)/shard_map/ppermute | solution.py:41
  132.5 11.8 %collective-permute-start.21 = (bf16[64,3328]{1,0:T(8,128)(2,1)S(1)}, bf16[64,3328]{1,0:T(8,128)(2,1)S(1)}, u32[]{:S(2)}, u32[]{:S(2)}) collective-permute-start(bf16[64,3328]{1,0:T(8,128)(2,1)S(1)} %get-tuple-element.117), channel_id=1, source_target_pairs={{0,32},{1,33},{2,34},{3,35},{16,48},{17,49},{18,50},{19,51},{32,64... | collective-permute-start | bytes 1277960 | tf_op jit(solution)/shard_map/ppermute | solution.py:41
  132.6 11.7 %collective-permute-start.22 = (bf16[64,3328]{1,0:T(8,128)(2,1)S(1)}, bf16[64,3328]{1,0:T(8,128)(2,1)S(1)}, u32[]{:S(2)}, u32[]{:S(2)}) collective-permute-start(bf16[64,3328]{1,0:T(8,128)(2,1)S(1)} %get-tuple-element.119), channel_id=1, source_target_pairs={{0,96},{1,97},{2,98},{3,99},{16,112},{17,113},{18,114},{19,115},{3... | collective-permute-start | bytes 1277960 | tf_op jit(solution)/shard_map/ppermute | solution.py:41
  144.7 22.3 %collective-permute-start.28 = (bf16[128,3328]{1,0:T(8,128)(2,1)S(1)}, bf16[128,3328]{1,0:T(8,128)(2,1)S(1)}, u32[]{:S(2)}, u32[]{:S(2)}) collective-permute-start(bf16[128,3328]{1,0:T(8,128)(2,1)S(1)} %get-tuple-element.135), channel_id=1, source_target_pairs={{0,32},{1,33},{2,34},{3,35},{16,48},{17,49},{18,50},{19,51},{32,64... | collective-permute-start | bytes 2555912 | tf_op jit(solution)/shard_map/ppermute | solution.py:41
  144.8 22.2 %collective-permute-start.29 = (bf16[128,3328]{1,0:T(8,128)(2,1)S(1)}, bf16[128,3328]{1,0:T(8,128)(2,1)S(1)}, u32[]{:S(2)}, u32[]{:S(2)}) collective-permute-start(bf16[128,3328]{1,0:T(8,128)(2,1)S(1)} %get-tuple-element.136), channel_id=1, source_target_pairs={{0,96},{1,97},{2,98},{3,99},{16,112},{17,113},{18,114},{19,115},{3... | collective-permute-start | bytes 2555912 | tf_op jit(solution)/shard_map/ppermute | solution.py:41
  148.0 16.4 %collective-permute-start.30 = (bf16[64,3328]{1,0:T(8,128)(2,1)S(1)}, bf16[64,3328]{1,0:T(8,128)(2,1)S(1)}, u32[]{:S(2)}, u32[]{:S(2)}) collective-permute-start(bf16[64,3328]{1,0:T(8,128)(2,1)S(1)} %get-tuple-element.138), channel_id=1, source_target_pairs={{0,16},{1,17},{2,18},{3,19},{16,0},{17,1},{18,2},{19,3},{32,48},{3... | collective-permute-start | bytes 1277960 | tf_op jit(solution)/shard_map/ppermute | solution.py:41
  157.8 12.5 %collective-permute-start.26 = (bf16[32,3328]{1,0:T(8,128)(2,1)S(1)}, bf16[32,3328]{1,0:T(8,128)(2,1)S(1)}, u32[]{:S(2)}, u32[]{:S(2)}) collective-permute-start(bf16[32,3328]{1,0:T(8,128)(2,1)S(1)} %get-tuple-element.131), channel_id=1, source_target_pairs={{0,32},{1,33},{2,34},{3,35},{16,48},{17,49},{18,50},{19,51},{32,64... | collective-permute-start | bytes 638984 | tf_op jit(solution)/shard_map/ppermute | solution.py:41
  157.9 12.4 %collective-permute-start.27 = (bf16[32,3328]{1,0:T(8,128)(2,1)S(1)}, bf16[32,3328]{1,0:T(8,128)(2,1)S(1)}, u32[]{:S(2)}, u32[]{:S(2)}) collective-permute-start(bf16[32,3328]{1,0:T(8,128)(2,1)S(1)} %get-tuple-element.133), channel_id=1, source_target_pairs={{0,96},{1,97},{2,98},{3,99},{16,112},{17,113},{18,114},{19,115},{3... | collective-permute-start | bytes 638984 | tf_op jit(solution)/shard_map/ppermute | solution.py:41
  167.7 11.0 %collective-permute-start.33 = (bf16[64,3328]{1,0:T(8,128)(2,1)S(1)}, bf16[64,3328]{1,0:T(8,128)(2,1)S(1)}, u32[]{:S(2)}, u32[]{:S(2)}) collective-permute-start(bf16[64,3328]{1,0:T(8,128)(2,1)S(1)} %get-tuple-element.147), channel_id=1, source_target_pairs={{0,16},{1,17},{2,18},{3,19},{16,0},{17,1},{18,2},{19,3},{32,48},{3... | collective-permute-start | bytes 1277960 | tf_op jit(solution)/shard_map/ppermute | solution.py:41
  170.5 10.9 %collective-permute-start.31 = (bf16[64,3328]{1,0:T(8,128)(2,1)S(1)}, bf16[64,3328]{1,0:T(8,128)(2,1)S(1)}, u32[]{:S(2)}, u32[]{:S(2)}) collective-permute-start(bf16[64,3328]{1,0:T(8,128)(2,1)S(1)} %get-tuple-element.144), channel_id=1, source_target_pairs={{0,32},{1,33},{2,34},{3,35},{16,48},{17,49},{18,50},{19,51},{32,64... | collective-permute-start | bytes 1277960 | tf_op jit(solution)/shard_map/ppermute | solution.py:41
  170.6 10.8 %collective-permute-start.32 = (bf16[64,3328]{1,0:T(8,128)(2,1)S(1)}, bf16[64,3328]{1,0:T(8,128)(2,1)S(1)}, u32[]{:S(2)}, u32[]{:S(2)}) collective-permute-start(bf16[64,3328]{1,0:T(8,128)(2,1)S(1)} %get-tuple-element.145), channel_id=1, source_target_pairs={{0,96},{1,97},{2,98},{3,99},{16,112},{17,113},{18,114},{19,115},{3... | collective-permute-start | bytes 1277960 | tf_op jit(solution)/shard_map/ppermute | solution.py:41
  (20 other events, 186.4 us)

commit v2 on v1

--- a/solution.py
+++ b/solution.py
@@ -12,14 +12,14 @@
 F32 = jnp.float32
 BF16 = jnp.bfloat16
 PARTS = (32, 96)
-GATHERS = (("a", 0, 0, 32), ("b", 1, 0, 32), ("c", 1, 32, 64))
+GATHERS = (("a", 0, 0, 32, False), ("b", 1, 0, 96, True))
 CHUNKS = (
     (0, 32, True, "a", 0),
     (1, 32, True, "b", 0),
-    (2, 32, False, "c", 0),
-    (3, 32, True, "c", 32),
+    (2, 32, False, "b", 32),
+    (3, 32, True, "b", 64),
 )
-ORDER = ("a", "w", "b", "a", 0, "b", "c", 0, 1, 0, "c", 1, 2, 3, 0, 1, 3, 2, 1, 3, 2, 3, 2)
+ORDER = ("a", "w", "b", "a", 0, "b", 0, "b", 1, 0, 2, 1, 3, 0, 1, 3, 2, 1, 3, 2, 3, 2)
 
 
 def place(x, y, z, core):
@@ -454,12 +454,21 @@
     )
 
 
-def gather_steps(part, paired, first, rows, kept):
+def gather_steps(part, paired, first, rows, relay, kept):
     token = yield
     block, token = join(token, (part, first, rows), (paired, first, rows))
     token = yield token
-    arrived = [send(block, move) for move in (x_down, x_across, x_up)]
-    mine, token = join(token, *((array, 0, 2 * rows) for array in (block, *arrived)))
+    above, below = send(block, x_down), send(block, x_up)
+    if relay:
+        low, token = join(token, (below, 0, rows))
+        high, token = join(token, (above, rows, rows))
+        token = yield token
+        across = ((send(low, x_up), 0, rows), (send(high, x_down), 0, rows))
+    else:
+        across = ((send(block, x_across), 0, 2 * rows),)
+    mine, token = join(
+        token, (block, 0, 2 * rows), (above, 0, 2 * rows), *across, (below, 0, 2 * rows)
+    )
     kept.extend((mine, send(mine, other_core)))
     yield token
 
@@ -515,9 +524,9 @@
         yield token
 
     steps["w"] = weight_steps()
-    for name, part, first, rows in GATHERS:
+    for name, part, first, rows, relay in GATHERS:
         kept[name] = []
-        steps[name] = gather_steps(*pairs[part], first, rows, kept[name])
+        steps[name] = gather_steps(*pairs[part], first, rows, relay, kept[name])
     first = 0
     for name, n, y_first, part, start in CHUNKS:
 

time: 198 us -> 192 us (0.970)
  waiting for transfers between devices: 46.6 us -> 41 us
  blocking collectives: 13.5 us -> 15.6 us
  starting transfers between devices: 53.1 us -> 51.1 us
    ppermute x34 -> x31, waiting for transfers between devices: 46.6 us -> 41 us  [send(): return lax.ppermute(value, ('row', 'col'), route(move))]
    all_to_all x1, blocking collectives: 13.5 us -> 15.6 us  [per_device(): lax.all_to_all(terms.reshape(n_row, tenants // n_row, ff), 'row', 0, 0)]
    ppermute x34 -> x31, starting transfers between devices: 53.1 us -> 51.1 us  [send(): return lax.ppermute(value, ('row', 'col'), route(move))]
    unnamed x36 -> x32, local copies, waits for them, and re-layouts: 4.32 us -> 4.6 us
  transfers between devices with their start and end apart: 34 -> 31, of which waited for: 10 -> 13; matrix products, arithmetic and copies ran while one was open for 0% -> 0% of each run, Pallas kernels for 38% -> 39%
where the time goes in v2:
time: 192 us
  Pallas kernels  77.8 us (41%)
  starting transfers between devices  51.1 us (27%)
  waiting for transfers between devices  41 us (21%)
  blocking collectives  15.6 us (8%)
  local copies, waits for them, and re-layouts  4.6 us (2%)
    pallas_call x24, Pallas kernels, chained(): pl.pallas_call(with_token, grid=grid, in_specs=[*in_specs, anywhere()], o...  77.8 us
    ppermute x31, starting transfers between devices, send(): return lax.ppermute(value, ('row', 'col'), route(move))  51.1 us
    ppermute x31, waiting for transfers between devices, send(): return lax.ppermute(value, ('row', 'col'), route(move))  41 us
    all_to_all x1, blocking collectives, per_device(): lax.all_to_all(terms.reshape(n_row, tenants // n_row, ff), 'row', 0, 0)  15.6 us
    unnamed x32, local copies, waits for them, and re-layouts  4.6 us
  transfers between devices with their start and end apart: 31, of which 13 were waited for; matrix products, arithmetic and copies ran while one was open for 0% of the time, Pallas kernels for 39%

profile of v2, /device:TPU:0, one launch (start us, length us, event | category | flops | bytes accessed | tf_op | source)
XLA Modules:
  0.0 191.8 jit_solution(12498492711309683499)
XLA Ops:
  3.0 2.1 %collective-permute-start.1 = (bf16[32,2048]{1,0:T(8,128)(2,1)S(1)}, bf16[32,2048]{1,0:T(8,128)(2,1)S(1)}, u32[]{:S(2)}, u32[]{:S(2)}) collective-permute-start(bf16[32,2048]{1,0:T(8,128)(2,1)S(1)} %get-tuple-element.81.refs_0_), channel_id=1, source_target_pairs={{0,2},{1,3},{2,0},{3,1},{16,18},{17,19},{18,16},{19,17},{32,34},{3... | collective-permute-start | bytes 393224 | tf_op jit(solution)/shard_map/ppermute | solution.py:41
  5.2 4.3 %collective-permute-done.1.refs_1_ = bf16[32,2048]{1,0:T(8,128)(2,1)S(1)} collective-permute-done((bf16[32,2048]{1,0:T(8,128)(2,1)S(1)}, bf16[32,2048]{1,0:T(8,128)(2,1)S(1)}, u32[]{:S(2)}, u32[]{:S(2)}) %collective-permute-start.1) | collective-permute-done | bytes 131104 | tf_op jit(solution)/shard_map/ppermute | solution.py:41
  11.1 2.7 %collective-permute-start.5 = (bf16[64,2048]{1,0:T(8,128)(2,1)S(1)}, bf16[64,2048]{1,0:T(8,128)(2,1)S(1)}, u32[]{:S(2)}, u32[]{:S(2)}) collective-permute-start(bf16[64,2048]{1,0:T(8,128)(2,1)S(1)} %get-tuple-element.86.refs_0_), channel_id=1, source_target_pairs={{0,8},{1,9},{2,10},{3,11},{16,24},{17,25},{18,26},{19,27},{32,40},... | collective-permute-start | bytes 786440 | tf_op jit(solution)/shard_map/ppermute | solution.py:41
  15.3 10.6 %dequantize.1 = (bf16[13,2048,256]{2,1,0:T(8,128)(2,1)}, f32[8,128]{1,0:T(8,128)S(1)}) custom-call(s32[13,256,1024]{2,1,0:T(8,128)} %bitcast.17, f32[26,1,2048]{2,1,0:T(1,128)S(1)} %get-tuple-element.80.refs_1_, f32[8,128]{1,0:T(8,128)S(1)} %get-tuple-element.83.refs_2_), custom_call_target="tpu_custom_call" | custom-call | flops 11000000512 | bytes 1 | tf_op jit(solution)/shard_map/dequantize/pallas_call | solution.py:95
  26.9 2.6 %collective-permute-start.2 = (bf16[192,2048]{1,0:T(8,128)(2,1)S(1)}, bf16[192,2048]{1,0:T(8,128)(2,1)S(1)}, u32[]{:S(2)}, u32[]{:S(2)}) collective-permute-start(bf16[192,2048]{1,0:T(8,128)(2,1)S(1)} %get-tuple-element.85.refs_0_), channel_id=1, source_target_pairs={{0,12},{1,13},{2,14},{3,15},{16,28},{17,29},{18,30},{19,31},{32,44... | collective-permute-start | bytes 2359304 | tf_op jit(solution)/shard_map/ppermute | solution.py:41
  30.5 13.8 %project.4 = (bf16[64,3328]{1,0:T(8,128)(2,1)S(1)}, bf16[64,3328]{1,0:T(8,128)(2,1)S(1)}, bf16[128,3328]{1,0:T(8,128)(2,1)S(1)}, bf16[128,3328]{1,0:T(8,128)(2,1...) custom-call(s32[2]{0:T(128)S(1)} %pad_add_fusion.refs_0_, bf16[256,2048]{1,0:T(8,128)(2,1)} %copy-done.13, ...), custom_call_target="tpu_custom_call" | custom-call | flops 13958643712 | bytes 1 | tf_op jit(solution)/shard_map/project/pallas_call | solution.py:95
  47.7 2.8 %collective-permute-start.9 = (bf16[96,2048]{1,0:T(8,128)(2,1)S(1)}, bf16[96,2048]{1,0:T(8,128)(2,1)S(1)}, u32[]{:S(2)}, u32[]{:S(2)}) collective-permute-start(bf16[96,2048]{1,0:T(8,128)(2,1)S(1)} %get-tuple-element.94), channel_id=1, source_target_pairs={{0,12},{1,13},{2,14},{3,15},{16,28},{17,29},{18,30},{19,31},{32,44... | collective-permute-start | bytes 1179656 | tf_op jit(solution)/shard_map/ppermute | solution.py:41
  50.5 6.8 %collective-permute-done.10.refs_1_ = bf16[64,3328]{1,0:T(8,128)(2,1)S(1)} collective-permute-done((bf16[64,3328]{1,0:T(8,128)(2,1)S(1)}, bf16[64,3328]{1,0:T(8,128)(2,1)S(1)}, u32[]{:S(2)}, u32[]{:S(2)}) %collective-permute-start.10) | collective-permute-done | bytes 426016 | tf_op jit(solution)/shard_map/ppermute | solution.py:41
  58.4 3.4 %collective-permute-done.8.refs_2_ = bf16[96,2048]{1,0:T(8,128)(2,1)S(1)} collective-permute-done((bf16[96,2048]{1,0:T(8,128)(2,1)S(1)}, bf16[96,2048]{1,0:T(8,128)(2,1)S(1)}, u32[]{:S(2)}, u32[]{:S(2)}) %collective-permute-start.8) | collective-permute-done | bytes 393248 | tf_op jit(solution)/shard_map/ppermute | solution.py:41
  63.8 1.7 collective-permute-start.14
  65.4 2.3 %collective-permute-done.12.refs_2_ = bf16[768,2048]{1,0:T(8,128)(2,1)S(1)} collective-permute-done((bf16[768,2048]{1,0:T(8,128)(2,1)S(1)}, bf16[768,2048]{1,0:T(8,128)(2,1)S(1)}, u32[]{:S(2)}, u32[]{:S(2)}) %collective-permute-start.12) | collective-permute-done | bytes 3145760 | tf_op jit(solution)/shard_map/ppermute | solution.py:41
  69.4 13.8 %project.5 = (bf16[64,3328]{1,0:T(8,128)(2,1)S(1)}, bf16[64,3328]{1,0:T(8,128)(2,1)S(1)}, bf16[128,3328]{1,0:T(8,128)(2,1)S(1)}, bf16[128,3328]{1,0:T(8,128)(2,1...) custom-call(s32[2]{0:T(128)S(1)} %pad_add_fusion.refs_0_, bf16[768,2048]{1,0:T(8,128)(2,1)} %copy-done.12, ...), custom_call_target="tpu_custom_call" | custom-call | flops 13958643712 | bytes 1 | tf_op jit(solution)/shard_map/project/pallas_call | solution.py:95
  85.4 4.0 %collective-permute-start.22 = (bf16[64,3328]{1,0:T(8,128)(2,1)S(1)}, bf16[64,3328]{1,0:T(8,128)(2,1)S(1)}, u32[]{:S(2)}, u32[]{:S(2)}) collective-permute-start(bf16[64,3328]{1,0:T(8,128)(2,1)S(1)} %get-tuple-element.124), channel_id=1, source_target_pairs={{0,16},{1,17},{2,18},{3,19},{16,0},{17,1},{18,2},{19,3},{32,48},{3... | collective-permute-start | bytes 1277960 | tf_op jit(solution)/shard_map/ppermute | solution.py:41
  92.6 13.2 %project.6 = (bf16[256,3328]{1,0:T(8,128)(2,1)S(1)}, bf16[256,3328]{1,0:T(8,128)(2,1)}, f32[8,128]{1,0:T(8,128)S(1)}) custom-call(s32[2]{0:T(128)S(1)} %pad_add_fusion.refs_0_, bf16[768,2048]{1,0:T(8,128)(2,1)} %copy-done.12, bf16[768,2048]{1,0:T(8,128)(2,1)} %copy-done.14, bf16[13,2048,256]{2,1,0:T(8,128)(2,1)} %get-tuple-element.89.refs_3_, ...), custom_call_target="tpu_custom_call" | custom-call | flops 13958643712 | bytes 1 | tf_op jit(solution)/shard_map/project/pallas_call | solution.py:95
  107.0 2.9 %collective-permute-start.21 = (bf16[128,3328]{1,0:T(8,128)(2,1)S(1)}, bf16[128,3328]{1,0:T(8,128)(2,1)S(1)}, u32[]{:S(2)}, u32[]{:S(2)}) collective-permute-start(bf16[128,3328]{1,0:T(8,128)(2,1)S(1)} %get-tuple-element.122), channel_id=1, source_target_pairs={{0,96},{1,97},{2,98},{3,99},{16,112},{17,113},{18,114},{19,115},{3... | collective-permute-start | bytes 2555912 | tf_op jit(solution)/shard_map/ppermute | solution.py:41
  109.8 13.8 %project.7 = (bf16[64,3328]{1,0:T(8,128)(2,1)S(1)}, bf16[64,3328]{1,0:T(8,128)(2,1)S(1)}, bf16[128,3328]{1,0:T(8,128)(2,1)S(1)}, bf16[128,3328]{1,0:T(8,128)(2,1...) custom-call(s32[2]{0:T(128)S(1)} %pad_add_fusion.refs_0_, bf16[768,2048]{1,0:T(8,128)(2,1)} %copy-done.12, ...), custom_call_target="tpu_custom_call" | custom-call | flops 13958643712 | bytes 1 | tf_op jit(solution)/shard_map/project/pallas_call | solution.py:95
  123.8 3.2 %collective-permute-start.19 = (bf16[64,3328]{1,0:T(8,128)(2,1)S(1)}, bf16[64,3328]{1,0:T(8,128)(2,1)S(1)}, u32[]{:S(2)}, u32[]{:S(2)}) collective-permute-start(bf16[64,3328]{1,0:T(8,128)(2,1)S(1)} %get-tuple-element.119), channel_id=1, source_target_pairs={{0,96},{1,97},{2,98},{3,99},{16,112},{17,113},{18,114},{19,115},{3... | collective-permute-start | bytes 1277960 | tf_op jit(solution)/shard_map/ppermute | solution.py:41
  127.0 1.8 finish.4
  129.7 6.9 %collective-permute-done.18.refs_1_ = bf16[64,3328]{1,0:T(8,128)(2,1)S(1)} collective-permute-done((bf16[64,3328]{1,0:T(8,128)(2,1)S(1)}, bf16[64,3328]{1,0:T(8,128)(2,1)S(1)}, u32[]{:S(2)}, u32[]{:S(2)}) %collective-permute-start.18) | collective-permute-done | bytes 426016 | tf_op jit(solution)/shard_map/ppermute | solution.py:41
  137.2 3.2 %collective-permute-start.26 = (bf16[128,3328]{1,0:T(8,128)(2,1)S(1)}, bf16[128,3328]{1,0:T(8,128)(2,1)S(1)}, u32[]{:S(2)}, u32[]{:S(2)}) collective-permute-start(bf16[128,3328]{1,0:T(8,128)(2,1)S(1)} %get-tuple-element.136), channel_id=1, source_target_pairs={{0,96},{1,97},{2,98},{3,99},{16,112},{17,113},{18,114},{19,115},{3... | collective-permute-start | bytes 2555912 | tf_op jit(solution)/shard_map/ppermute | solution.py:41
  140.4 3.2 %collective-permute-start.27 = (bf16[64,3328]{1,0:T(8,128)(2,1)S(1)}, bf16[64,3328]{1,0:T(8,128)(2,1)S(1)}, u32[]{:S(2)}, u32[]{:S(2)}) collective-permute-start(bf16[64,3328]{1,0:T(8,128)(2,1)S(1)} %get-tuple-element.138), channel_id=1, source_target_pairs={{0,16},{1,17},{2,18},{3,19},{16,0},{17,1},{18,2},{19,3},{32,48},{3... | collective-permute-start | bytes 1277960 | tf_op jit(solution)/shard_map/ppermute | solution.py:41
  143.6 4.0 %collective-permute-done.15.refs_1_ = bf16[256,3328]{1,0:T(8,128)(2,1)S(1)} collective-permute-done((bf16[256,3328]{1,0:T(8,128)(2,1)S(1)}, bf16[256,3328]{1,0:T(8,128)(2,1)S(1)}, u32[]{:S(2)}, u32[]{:S(2)}) %collective-permute-start.15) | collective-permute-done | bytes 1703968 | tf_op jit(solution)/shard_map/ppermute | solution.py:41
  148.9 2.9 %collective-permute-start.24 = (bf16[32,3328]{1,0:T(8,128)(2,1)S(1)}, bf16[32,3328]{1,0:T(8,128)(2,1)S(1)}, u32[]{:S(2)}, u32[]{:S(2)}) collective-permute-start(bf16[32,3328]{1,0:T(8,128)(2,1)S(1)} %get-tuple-element.133), channel_id=1, source_target_pairs={{0,96},{1,97},{2,98},{3,99},{16,112},{17,113},{18,114},{19,115},{3... | collective-permute-start | bytes 638984 | tf_op jit(solution)/shard_map/ppermute | solution.py:41
  151.7 2.8 %collective-permute-done.27.refs_4_ = bf16[64,3328]{1,0:T(8,128)(2,1)S(1)} collective-permute-done((bf16[64,3328]{1,0:T(8,128)(2,1)S(1)}, bf16[64,3328]{1,0:T(8,128)(2,1)S(1)}, u32[]{:S(2)}, u32[]{:S(2)}) %collective-permute-start.27) | collective-permute-done | bytes 426016 | tf_op jit(solution)/shard_map/ppermute | solution.py:41
  154.5 1.9 finish.5
  156.4 3.6 %collective-permute-done.25.refs_1_ = bf16[128,3328]{1,0:T(8,128)(2,1)S(1)} collective-permute-done((bf16[128,3328]{1,0:T(8,128)(2,1)S(1)}, bf16[128,3328]{1,0:T(8,128)(2,1)S(1)}, u32[]{:S(2)}, u32[]{:S(2)}) %collective-permute-start.25) | collective-permute-done | bytes 852000 | tf_op jit(solution)/shard_map/ppermute | solution.py:41
  160.7 3.2 %collective-permute-start.30 = (bf16[64,3328]{1,0:T(8,128)(2,1)S(1)}, bf16[64,3328]{1,0:T(8,128)(2,1)S(1)}, u32[]{:S(2)}, u32[]{:S(2)}) collective-permute-start(bf16[64,3328]{1,0:T(8,128)(2,1)S(1)} %get-tuple-element.147), channel_id=1, source_target_pairs={{0,16},{1,17},{2,18},{3,19},{16,0},{17,1},{18,2},{19,3},{32,48},{3... | collective-permute-start | bytes 1277960 | tf_op jit(solution)/shard_map/ppermute | solution.py:41
  165.3 2.2 %collective-permute-start.29 = (bf16[64,3328]{1,0:T(8,128)(2,1)S(1)}, bf16[64,3328]{1,0:T(8,128)(2,1)S(1)}, u32[]{:S(2)}, u32[]{:S(2)}) collective-permute-start(bf16[64,3328]{1,0:T(8,128)(2,1)S(1)} %get-tuple-element.145), channel_id=1, source_target_pairs={{0,96},{1,97},{2,98},{3,99},{16,112},{17,113},{18,114},{19,115},{3... | collective-permute-start | bytes 1277960 | tf_op jit(solution)/shard_map/ppermute | solution.py:41
  167.5 2.9 %collective-permute-done.30.refs_4_ = bf16[64,3328]{1,0:T(8,128)(2,1)S(1)} collective-permute-done((bf16[64,3328]{1,0:T(8,128)(2,1)S(1)}, bf16[64,3328]{1,0:T(8,128)(2,1)S(1)}, u32[]{:S(2)}, u32[]{:S(2)}) %collective-permute-start.30) | collective-permute-done | bytes 426016 | tf_op jit(solution)/shard_map/ppermute | solution.py:41
  170.4 1.9 finish.6
  173.6 1.9 finish.7
  175.5 15.6 %all_to_all.5 = bf16[8,8,3328]{2,1,0:T(8,128)(2,1)S(1)} all-to-all(bf16[8,8,3328]{2,1,0:T(8,128)(2,1)S(1)} %bitcast.11), channel_id=1, replica_groups=mesh['row'=8,'col'=16] {'row'}, dimensions={0} | all-to-all | bytes 851968 | tf_op jit(solution)/shard_map/all_to_all | solution.py:547
  (90 shorter events, 28.9 us)
Async XLA Ops:
  3.0 6.4 %collective-permute-start.1 = (bf16[32,2048]{1,0:T(8,128)(2,1)S(1)}, bf16[32,2048]{1,0:T(8,128)(2,1)S(1)}, u32[]{:S(2)}, u32[]{:S(2)}) collective-permute-start(bf16[32,2048]{1,0:T(8,128)(2,1)S(1)} %get-tuple-element.81.refs_0_), channel_id=1, source_target_pairs={{0,2},{1,3},{2,0},{3,1},{16,18},{17,19},{18,16},{19,17},{32,34},{3... | collective-permute-start | bytes 393224 | tf_op jit(solution)/shard_map/ppermute | solution.py:41
  5.1 20.8 %collective-permute-start = (bf16[96,2048]{1,0:T(8,128)(2,1)S(1)}, bf16[96,2048]{1,0:T(8,128)(2,1)S(1)}, u32[]{:S(2)}, u32[]{:S(2)}) collective-permute-start(bf16[96,2048]{1,0:T(8,128)(2,1)S(1)} %get-tuple-element.79.refs_0_), channel_id=1, source_target_pairs={{0,2},{1,3},{2,0},{3,1},{16,18},{17,19},{18,16},{19,17},{32,34},{3... | collective-permute-start | bytes 1179656 | tf_op jit(solution)/shard_map/ppermute | solution.py:41
  9.5 16.5 %collective-permute-start.6 = (bf16[64,2048]{1,0:T(8,128)(2,1)S(1)}, bf16[64,2048]{1,0:T(8,128)(2,1)S(1)}, u32[]{:S(2)}, u32[]{:S(2)}) collective-permute-start(bf16[64,2048]{1,0:T(8,128)(2,1)S(1)} %get-tuple-element.86.refs_0_), channel_id=1, source_target_pairs={{0,4},{1,5},{2,6},{3,7},{16,20},{17,21},{18,22},{19,23},{32,36},{3... | collective-permute-start | bytes 786440 | tf_op jit(solution)/shard_map/ppermute | solution.py:41
  11.1 14.8 %collective-permute-start.5 = (bf16[64,2048]{1,0:T(8,128)(2,1)S(1)}, bf16[64,2048]{1,0:T(8,128)(2,1)S(1)}, u32[]{:S(2)}, u32[]{:S(2)}) collective-permute-start(bf16[64,2048]{1,0:T(8,128)(2,1)S(1)} %get-tuple-element.86.refs_0_), channel_id=1, source_target_pairs={{0,8},{1,9},{2,10},{3,11},{16,24},{17,25},{18,26},{19,27},{32,40},... | collective-permute-start | bytes 786440 | tf_op jit(solution)/shard_map/ppermute | solution.py:41
  13.9 12.1 %collective-permute-start.4 = (bf16[64,2048]{1,0:T(8,128)(2,1)S(1)}, bf16[64,2048]{1,0:T(8,128)(2,1)S(1)}, u32[]{:S(2)}, u32[]{:S(2)}) collective-permute-start(bf16[64,2048]{1,0:T(8,128)(2,1)S(1)} %get-tuple-element.86.refs_0_), channel_id=1, source_target_pairs={{0,12},{1,13},{2,14},{3,15},{16,28},{17,29},{18,30},{19,31},{32,44... | collective-permute-start | bytes 786440 | tf_op jit(solution)/shard_map/ppermute | solution.py:41
  26.1 3.4 %collective-permute-start.7 = (bf16[256,2048]{1,0:T(8,128)(2,1)S(1)}, bf16[256,2048]{1,0:T(8,128)(2,1)S(1)}, u32[]{:S(2)}, u32[]{:S(2)}) collective-permute-start(bf16[256,2048]{1,0:T(8,128)(2,1)S(1)} %get-tuple-element.88.refs_1_), channel_id=1, source_target_pairs={{0,1},{1,0},{2,3},{3,2},{16,17},{17,16},{18,19},{19,18},{32,33},{3... | collective-permute-start | bytes 3145736 | tf_op jit(solution)/shard_map/ppermute | solution.py:41
  26.3 21.4 %collective-permute-start.3 = (bf16[192,2048]{1,0:T(8,128)(2,1)S(1)}, bf16[192,2048]{1,0:T(8,128)(2,1)S(1)}, u32[]{:S(2)}, u32[]{:S(2)}) collective-permute-start(bf16[192,2048]{1,0:T(8,128)(2,1)S(1)} %get-tuple-element.85.refs_0_), channel_id=1, source_target_pairs={{0,4},{1,5},{2,6},{3,7},{16,20},{17,21},{18,22},{19,23},{32,36},{3... | collective-permute-start | bytes 2359304 | tf_op jit(solution)/shard_map/ppermute | solution.py:41
  26.9 20.8 %collective-permute-start.2 = (bf16[192,2048]{1,0:T(8,128)(2,1)S(1)}, bf16[192,2048]{1,0:T(8,128)(2,1)S(1)}, u32[]{:S(2)}, u32[]{:S(2)}) collective-permute-start(bf16[192,2048]{1,0:T(8,128)(2,1)S(1)} %get-tuple-element.85.refs_0_), channel_id=1, source_target_pairs={{0,12},{1,13},{2,14},{3,15},{16,28},{17,29},{18,30},{19,31},{32,44... | collective-permute-start | bytes 2359304 | tf_op jit(solution)/shard_map/ppermute | solution.py:41
  44.3 13.0 %collective-permute-start.10 = (bf16[64,3328]{1,0:T(8,128)(2,1)S(1)}, bf16[64,3328]{1,0:T(8,128)(2,1)S(1)}, u32[]{:S(2)}, u32[]{:S(2)}) collective-permute-start(bf16[64,3328]{1,0:T(8,128)(2,1)S(1)} %get-tuple-element.96), channel_id=1, source_target_pairs={{0,32},{1,33},{2,34},{3,35},{16,48},{17,49},{18,50},{19,51},{32,64... | collective-permute-start | bytes 1277960 | tf_op jit(solution)/shard_map/ppermute | solution.py:41
  46.0 11.4 %collective-permute-start.11 = (bf16[64,3328]{1,0:T(8,128)(2,1)S(1)}, bf16[64,3328]{1,0:T(8,128)(2,1)S(1)}, u32[]{:S(2)}, u32[]{:S(2)}) collective-permute-start(bf16[64,3328]{1,0:T(8,128)(2,1)S(1)} %get-tuple-element.98), channel_id=1, source_target_pairs={{0,96},{1,97},{2,98},{3,99},{16,112},{17,113},{18,114},{19,115},{3... | collective-permute-start | bytes 1277960 | tf_op jit(solution)/shard_map/ppermute | solution.py:41
  47.7 10.7 %collective-permute-start.9 = (bf16[96,2048]{1,0:T(8,128)(2,1)S(1)}, bf16[96,2048]{1,0:T(8,128)(2,1)S(1)}, u32[]{:S(2)}, u32[]{:S(2)}) collective-permute-start(bf16[96,2048]{1,0:T(8,128)(2,1)S(1)} %get-tuple-element.94), channel_id=1, source_target_pairs={{0,12},{1,13},{2,14},{3,15},{16,28},{17,29},{18,30},{19,31},{32,44... | collective-permute-start | bytes 1179656 | tf_op jit(solution)/shard_map/ppermute | solution.py:41
  50.5 11.3 %collective-permute-start.8 = (bf16[96,2048]{1,0:T(8,128)(2,1)S(1)}, bf16[96,2048]{1,0:T(8,128)(2,1)S(1)}, u32[]{:S(2)}, u32[]{:S(2)}) collective-permute-start(bf16[96,2048]{1,0:T(8,128)(2,1)S(1)} %get-tuple-element.92), channel_id=1, source_target_pairs={{0,4},{1,5},{2,6},{3,7},{16,20},{17,21},{18,22},{19,23},{32,36},{3... | collective-permute-start | bytes 1179656 | tf_op jit(solution)/shard_map/ppermute | solution.py:41
  62.0 5.7 %collective-permute-start.12 = (bf16[768,2048]{1,0:T(8,128)(2,1)S(1)}, bf16[768,2048]{1,0:T(8,128)(2,1)S(1)}, u32[]{:S(2)}, u32[]{:S(2)}) collective-permute-start(bf16[768,2048]{1,0:T(8,128)(2,1)S(1)} %get-tuple-element.101.refs_1_), channel_id=1, source_target_pairs={{0,1},{1,0},{2,3},{3,2},{16,17},{17,16},{18,19},{19,18},{32,33},{3... | collective-permute-start | bytes 9437192 | tf_op jit(solution)/shard_map/ppermute | solution.py:41
  62.1 22.6 %collective-permute-start.13 = (bf16[128,3328]{1,0:T(8,128)(2,1)S(1)}, bf16[128,3328]{1,0:T(8,128)(2,1)S(1)}, u32[]{:S(2)}, u32[]{:S(2)}) collective-permute-start(bf16[128,3328]{1,0:T(8,128)(2,1)S(1)} %get-tuple-element.103), channel_id=1, source_target_pairs={{0,32},{1,33},{2,34},{3,35},{16,48},{17,49},{18,50},{19,51},{32,64... | collective-permute-start | bytes 2555912 | tf_op jit(solution)/shard_map/ppermute | solution.py:41
  63.8 21.0 %collective-permute-start.14 = (bf16[128,3328]{1,0:T(8,128)(2,1)S(1)}, bf16[128,3328]{1,0:T(8,128)(2,1)S(1)}, u32[]{:S(2)}, u32[]{:S(2)}) collective-permute-start(bf16[128,3328]{1,0:T(8,128)(2,1)S(1)} %get-tuple-element.104), channel_id=1, source_target_pairs={{0,96},{1,97},{2,98},{3,99},{16,112},{17,113},{18,114},{19,115},{3... | collective-permute-start | bytes 2555912 | tf_op jit(solution)/shard_map/ppermute | solution.py:41
  85.4 38.3 %collective-permute-start.22 = (bf16[64,3328]{1,0:T(8,128)(2,1)S(1)}, bf16[64,3328]{1,0:T(8,128)(2,1)S(1)}, u32[]{:S(2)}, u32[]{:S(2)}) collective-permute-start(bf16[64,3328]{1,0:T(8,128)(2,1)S(1)} %get-tuple-element.124), channel_id=1, source_target_pairs={{0,16},{1,17},{2,18},{3,19},{16,0},{17,1},{18,2},{19,3},{32,48},{3... | collective-permute-start | bytes 1277960 | tf_op jit(solution)/shard_map/ppermute | solution.py:41
  89.4 16.6 %collective-permute-start.16 = (bf16[64,3328]{1,0:T(8,128)(2,1)S(1)}, bf16[64,3328]{1,0:T(8,128)(2,1)S(1)}, u32[]{:S(2)}, u32[]{:S(2)}) collective-permute-start(bf16[64,3328]{1,0:T(8,128)(2,1)S(1)} %get-tuple-element.111), channel_id=1, source_target_pairs={{0,32},{1,33},{2,34},{3,35},{16,48},{17,49},{18,50},{19,51},{32,64... | collective-permute-start | bytes 1277960 | tf_op jit(solution)/shard_map/ppermute | solution.py:41
  91.0 15.1 %collective-permute-start.17 = (bf16[64,3328]{1,0:T(8,128)(2,1)S(1)}, bf16[64,3328]{1,0:T(8,128)(2,1)S(1)}, u32[]{:S(2)}, u32[]{:S(2)}) collective-permute-start(bf16[64,3328]{1,0:T(8,128)(2,1)S(1)} %get-tuple-element.113), channel_id=1, source_target_pairs={{0,96},{1,97},{2,98},{3,99},{16,112},{17,113},{18,114},{19,115},{3... | collective-permute-start | bytes 1277960 | tf_op jit(solution)/shard_map/ppermute | solution.py:41
  105.9 41.7 %collective-permute-start.15 = (bf16[256,3328]{1,0:T(8,128)(2,1)S(1)}, bf16[256,3328]{1,0:T(8,128)(2,1)S(1)}, u32[]{:S(2)}, u32[]{:S(2)}) collective-permute-start(bf16[256,3328]{1,0:T(8,128)(2,1)S(1)} %get-tuple-element.109), channel_id=1, source_target_pairs={{0,16},{1,17},{2,18},{3,19},{16,0},{17,1},{18,2},{19,3},{32,48},{3... | collective-permute-start | bytes 5111816 | tf_op jit(solution)/shard_map/ppermute | solution.py:41
  106.5 22.6 %collective-permute-start.20 = (bf16[128,3328]{1,0:T(8,128)(2,1)S(1)}, bf16[128,3328]{1,0:T(8,128)(2,1)S(1)}, u32[]{:S(2)}, u32[]{:S(2)}) collective-permute-start(bf16[128,3328]{1,0:T(8,128)(2,1)S(1)} %get-tuple-element.121), channel_id=1, source_target_pairs={{0,32},{1,33},{2,34},{3,35},{16,48},{17,49},{18,50},{19,51},{32,64... | collective-permute-start | bytes 2555912 | tf_op jit(solution)/shard_map/ppermute | solution.py:41
  107.0 22.1 %collective-permute-start.21 = (bf16[128,3328]{1,0:T(8,128)(2,1)S(1)}, bf16[128,3328]{1,0:T(8,128)(2,1)S(1)}, u32[]{:S(2)}, u32[]{:S(2)}) collective-permute-start(bf16[128,3328]{1,0:T(8,128)(2,1)S(1)} %get-tuple-element.122), channel_id=1, source_target_pairs={{0,96},{1,97},{2,98},{3,99},{16,112},{17,113},{18,114},{19,115},{3... | collective-permute-start | bytes 2555912 | tf_op jit(solution)/shard_map/ppermute | solution.py:41
  123.7 12.9 %collective-permute-start.18 = (bf16[64,3328]{1,0:T(8,128)(2,1)S(1)}, bf16[64,3328]{1,0:T(8,128)(2,1)S(1)}, u32[]{:S(2)}, u32[]{:S(2)}) collective-permute-start(bf16[64,3328]{1,0:T(8,128)(2,1)S(1)} %get-tuple-element.117), channel_id=1, source_target_pairs={{0,32},{1,33},{2,34},{3,35},{16,48},{17,49},{18,50},{19,51},{32,64... | collective-permute-start | bytes 1277960 | tf_op jit(solution)/shard_map/ppermute | solution.py:41
  123.8 12.8 %collective-permute-start.19 = (bf16[64,3328]{1,0:T(8,128)(2,1)S(1)}, bf16[64,3328]{1,0:T(8,128)(2,1)S(1)}, u32[]{:S(2)}, u32[]{:S(2)}) collective-permute-start(bf16[64,3328]{1,0:T(8,128)(2,1)S(1)} %get-tuple-element.119), channel_id=1, source_target_pairs={{0,96},{1,97},{2,98},{3,99},{16,112},{17,113},{18,114},{19,115},{3... | collective-permute-start | bytes 1277960 | tf_op jit(solution)/shard_map/ppermute | solution.py:41
  129.7 17.9 %copy-start.2 = (bf16[256,3328]{1,0:T(8,128)(2,1)S(1)}, bf16[256,3328]{1,0:T(8,128)(2,1)}, u32[]{:S(2)}) copy-start(bf16[256,3328]{1,0:T(8,128)(2,1)} %get-tuple-element.108.refs_0_) | copy-start | bytes 5111812
  137.1 22.9 %collective-permute-start.25 = (bf16[128,3328]{1,0:T(8,128)(2,1)S(1)}, bf16[128,3328]{1,0:T(8,128)(2,1)S(1)}, u32[]{:S(2)}, u32[]{:S(2)}) collective-permute-start(bf16[128,3328]{1,0:T(8,128)(2,1)S(1)} %get-tuple-element.135), channel_id=1, source_target_pairs={{0,32},{1,33},{2,34},{3,35},{16,48},{17,49},{18,50},{19,51},{32,64... | collective-permute-start | bytes 2555912 | tf_op jit(solution)/shard_map/ppermute | solution.py:41
  137.2 22.9 %collective-permute-start.26 = (bf16[128,3328]{1,0:T(8,128)(2,1)S(1)}, bf16[128,3328]{1,0:T(8,128)(2,1)S(1)}, u32[]{:S(2)}, u32[]{:S(2)}) collective-permute-start(bf16[128,3328]{1,0:T(8,128)(2,1)S(1)} %get-tuple-element.136), channel_id=1, source_target_pairs={{0,96},{1,97},{2,98},{3,99},{16,112},{17,113},{18,114},{19,115},{3... | collective-permute-start | bytes 2555912 | tf_op jit(solution)/shard_map/ppermute | solution.py:41
  140.4 14.1 %collective-permute-start.27 = (bf16[64,3328]{1,0:T(8,128)(2,1)S(1)}, bf16[64,3328]{1,0:T(8,128)(2,1)S(1)}, u32[]{:S(2)}, u32[]{:S(2)}) collective-permute-start(bf16[64,3328]{1,0:T(8,128)(2,1)S(1)} %get-tuple-element.138), channel_id=1, source_target_pairs={{0,16},{1,17},{2,18},{3,19},{16,0},{17,1},{18,2},{19,3},{32,48},{3... | collective-permute-start | bytes 1277960 | tf_op jit(solution)/shard_map/ppermute | solution.py:41
  148.4 15.5 %collective-permute-start.23 = (bf16[32,3328]{1,0:T(8,128)(2,1)S(1)}, bf16[32,3328]{1,0:T(8,128)(2,1)S(1)}, u32[]{:S(2)}, u32[]{:S(2)}) collective-permute-start(bf16[32,3328]{1,0:T(8,128)(2,1)S(1)} %get-tuple-element.131), channel_id=1, source_target_pairs={{0,32},{1,33},{2,34},{3,35},{16,48},{17,49},{18,50},{19,51},{32,64... | collective-permute-start | bytes 638984 | tf_op jit(solution)/shard_map/ppermute | solution.py:41
  148.9 15.0 %collective-permute-start.24 = (bf16[32,3328]{1,0:T(8,128)(2,1)S(1)}, bf16[32,3328]{1,0:T(8,128)(2,1)S(1)}, u32[]{:S(2)}, u32[]{:S(2)}) collective-permute-start(bf16[32,3328]{1,0:T(8,128)(2,1)S(1)} %get-tuple-element.133), channel_id=1, source_target_pairs={{0,96},{1,97},{2,98},{3,99},{16,112},{17,113},{18,114},{19,115},{3... | collective-permute-start | bytes 638984 | tf_op jit(solution)/shard_map/ppermute | solution.py:41
  160.7 9.7 %collective-permute-start.30 = (bf16[64,3328]{1,0:T(8,128)(2,1)S(1)}, bf16[64,3328]{1,0:T(8,128)(2,1)S(1)}, u32[]{:S(2)}, u32[]{:S(2)}) collective-permute-start(bf16[64,3328]{1,0:T(8,128)(2,1)S(1)} %get-tuple-element.147), channel_id=1, source_target_pairs={{0,16},{1,17},{2,18},{3,19},{16,0},{17,1},{18,2},{19,3},{32,48},{3... | collective-permute-start | bytes 1277960 | tf_op jit(solution)/shard_map/ppermute | solution.py:41
  164.2 9.4 %collective-permute-start.28 = (bf16[64,3328]{1,0:T(8,128)(2,1)S(1)}, bf16[64,3328]{1,0:T(8,128)(2,1)S(1)}, u32[]{:S(2)}, u32[]{:S(2)}) collective-permute-start(bf16[64,3328]{1,0:T(8,128)(2,1)S(1)} %get-tuple-element.144), channel_id=1, source_target_pairs={{0,32},{1,33},{2,34},{3,35},{16,48},{17,49},{18,50},{19,51},{32,64... | collective-permute-start | bytes 1277960 | tf_op jit(solution)/shard_map/ppermute | solution.py:41
  165.3 8.3 %collective-permute-start.29 = (bf16[64,3328]{1,0:T(8,128)(2,1)S(1)}, bf16[64,3328]{1,0:T(8,128)(2,1)S(1)}, u32[]{:S(2)}, u32[]{:S(2)}) collective-permute-start(bf16[64,3328]{1,0:T(8,128)(2,1)S(1)} %get-tuple-element.145), channel_id=1, source_target_pairs={{0,96},{1,97},{2,98},{3,99},{16,112},{17,113},{18,114},{19,115},{3... | collective-permute-start | bytes 1277960 | tf_op jit(solution)/shard_map/ppermute | solution.py:41
  (15 other events, 122.5 us)

commit v3 on v2

--- a/solution.py
+++ b/solution.py
@@ -237,7 +237,7 @@
     def stores(i):
         at = pl.ds(pl.multiple_of(i * TILE, TILE), TILE)
         return [
-            pltpu.make_async_copy(o_v.at[pl.ds(start, size), at], out.at[:, at], o_sem.at[p, i])
+            pltpu.make_async_copy(o_v.at[pl.ds(start, size), at], out.at[:, at], o_sem.at[p])
             for p, (out, (start, size)) in enumerate(zip(outs, pieces))
         ]
 
@@ -255,15 +255,14 @@
                 pltpu.make_async_copy(
                     source.at[pl.ds(start, n), :],
                     g_v.at[pl.ds(at, n), :],
-                    g_sem.at[2 * p + other],
+                    g_sem,
                 )
             )
     fetch(0).start()
     for copy in gathers:
         copy.start()
     fetch(1).start()
-    for copy in gathers:
-        copy.wait()
+    pltpu.make_async_copy(g_v, g_v, g_sem).wait()
 
     def step(i, carry):
         fetch(i).wait()
@@ -280,12 +279,8 @@
 
     lax.fori_loop(0, tiles, step, 0)
 
-    def finish(i, carry):
-        for copy in stores(i):
-            copy.wait()
-        return carry
-
-    lax.fori_loop(0, tiles, finish, 0)
+    for p, (out, (start, size)) in enumerate(zip(outs, pieces)):
+        pltpu.make_async_copy(o_v.at[pl.ds(start, size)], out, o_sem.at[p]).wait()
 
 
 def project(token, here, mine, theirs, first, n, weight, blocks, pieces):
@@ -302,9 +297,9 @@
             pltpu.VMEM((16 * n, k), BF16),
             pltpu.VMEM((3, *weight.shape[1:]), BF16),
             pltpu.VMEM((16 * n, ff), BF16),
-            pltpu.SemaphoreType.DMA((16,)),
+            pltpu.SemaphoreType.DMA,
             pltpu.SemaphoreType.DMA((3,)),
-            pltpu.SemaphoreType.DMA((len(pieces), tiles)),
+            pltpu.SemaphoreType.DMA((len(pieces),)),
         ],
         mib=52,
         flops=4 * 16 * n * k * ff,

time: 192 us -> 190 us (0.990)
  Pallas kernels: 77.8 us -> 75.4 us
    pallas_call x24, Pallas kernels: 77.8 us -> 75.4 us  [chained(): pl.pallas_call(with_token, grid=grid, in_specs=[*in_specs, anywhere()], o...]
  transfers between devices with their start and end apart: 31 -> 31, of which waited for: 13 -> 14; matrix products, arithmetic and copies ran while one was open for 0% -> 0% of each run, Pallas kernels for 39% -> 38%
where the time goes in v3:
time: 190 us
  Pallas kernels  75.4 us (40%)
  starting transfers between devices  51.2 us (27%)
  waiting for transfers between devices  42.2 us (22%)
  blocking collectives  15 us (8%)
  local copies, waits for them, and re-layouts  4.6 us (2%)
    pallas_call x24, Pallas kernels, chained(): pl.pallas_call(with_token, grid=grid, in_specs=[*in_specs, anywhere()], o...  75.4 us
    ppermute x31, starting transfers between devices, send(): return lax.ppermute(value, ('row', 'col'), route(move))  51.2 us
    ppermute x31, waiting for transfers between devices, send(): return lax.ppermute(value, ('row', 'col'), route(move))  42.2 us
    all_to_all x1, blocking collectives, per_device(): lax.all_to_all(terms.reshape(n_row, tenants // n_row, ff), 'row', 0, 0)  15 us
    unnamed x32, local copies, waits for them, and re-layouts  4.6 us
  transfers between devices with their start and end apart: 31, of which 14 were waited for; matrix products, arithmetic and copies ran while one was open for 0% of the time, Pallas kernels for 38%

profile of v3, /device:TPU:0, one launch (start us, length us, event | category | flops | bytes accessed | tf_op | source)
XLA Modules:
  0.0 190.1 jit_solution(10737460929570790992)
XLA Ops:
  3.0 2.1 %collective-permute-start.1 = (bf16[32,2048]{1,0:T(8,128)(2,1)S(1)}, bf16[32,2048]{1,0:T(8,128)(2,1)S(1)}, u32[]{:S(2)}, u32[]{:S(2)}) collective-permute-start(bf16[32,2048]{1,0:T(8,128)(2,1)S(1)} %get-tuple-element.81.refs_0_), channel_id=1, source_target_pairs={{0,2},{1,3},{2,0},{3,1},{16,18},{17,19},{18,16},{19,17},{32,34},{3... | collective-permute-start | bytes 393224 | tf_op jit(solution)/shard_map/ppermute | solution.py:41
  5.2 4.3 %collective-permute-done.1.refs_1_ = bf16[32,2048]{1,0:T(8,128)(2,1)S(1)} collective-permute-done((bf16[32,2048]{1,0:T(8,128)(2,1)S(1)}, bf16[32,2048]{1,0:T(8,128)(2,1)S(1)}, u32[]{:S(2)}, u32[]{:S(2)}) %collective-permute-start.1) | collective-permute-done | bytes 131104 | tf_op jit(solution)/shard_map/ppermute | solution.py:41
  11.1 2.7 %collective-permute-start.5 = (bf16[64,2048]{1,0:T(8,128)(2,1)S(1)}, bf16[64,2048]{1,0:T(8,128)(2,1)S(1)}, u32[]{:S(2)}, u32[]{:S(2)}) collective-permute-start(bf16[64,2048]{1,0:T(8,128)(2,1)S(1)} %get-tuple-element.86.refs_0_), channel_id=1, source_target_pairs={{0,8},{1,9},{2,10},{3,11},{16,24},{17,25},{18,26},{19,27},{32,40},... | collective-permute-start | bytes 786440 | tf_op jit(solution)/shard_map/ppermute | solution.py:41
  15.3 10.6 %dequantize.1 = (bf16[13,2048,256]{2,1,0:T(8,128)(2,1)}, f32[8,128]{1,0:T(8,128)S(1)}) custom-call(s32[13,256,1024]{2,1,0:T(8,128)} %bitcast.17, f32[26,1,2048]{2,1,0:T(1,128)S(1)} %get-tuple-element.80.refs_1_, f32[8,128]{1,0:T(8,128)S(1)} %get-tuple-element.83.refs_2_), custom_call_target="tpu_custom_call" | custom-call | flops 11000000512 | bytes 1 | tf_op jit(solution)/shard_map/dequantize/pallas_call | solution.py:95
  26.9 2.6 %collective-permute-start.2 = (bf16[192,2048]{1,0:T(8,128)(2,1)S(1)}, bf16[192,2048]{1,0:T(8,128)(2,1)S(1)}, u32[]{:S(2)}, u32[]{:S(2)}) collective-permute-start(bf16[192,2048]{1,0:T(8,128)(2,1)S(1)} %get-tuple-element.85.refs_0_), channel_id=1, source_target_pairs={{0,12},{1,13},{2,14},{3,15},{16,28},{17,29},{18,30},{19,31},{32,44... | collective-permute-start | bytes 2359304 | tf_op jit(solution)/shard_map/ppermute | solution.py:41
  30.5 13.1 %project.4 = (bf16[64,3328]{1,0:T(8,128)(2,1)S(1)}, bf16[64,3328]{1,0:T(8,128)(2,1)S(1)}, bf16[128,3328]{1,0:T(8,128)(2,1)S(1)}, bf16[128,3328]{1,0:T(8,128)(2,1...) custom-call(s32[2]{0:T(128)S(1)} %pad_add_fusion.refs_0_, bf16[256,2048]{1,0:T(8,128)(2,1)} %copy-done.13, ...), custom_call_target="tpu_custom_call" | custom-call | flops 13958643712 | bytes 1 | tf_op jit(solution)/shard_map/project/pallas_call | solution.py:95
  47.5 3.0 %collective-permute-start.9 = (bf16[96,2048]{1,0:T(8,128)(2,1)S(1)}, bf16[96,2048]{1,0:T(8,128)(2,1)S(1)}, u32[]{:S(2)}, u32[]{:S(2)}) collective-permute-start(bf16[96,2048]{1,0:T(8,128)(2,1)S(1)} %get-tuple-element.94), channel_id=1, source_target_pairs={{0,12},{1,13},{2,14},{3,15},{16,28},{17,29},{18,30},{19,31},{32,44... | collective-permute-start | bytes 1179656 | tf_op jit(solution)/shard_map/ppermute | solution.py:41
  50.5 6.1 %collective-permute-done.10.refs_1_ = bf16[64,3328]{1,0:T(8,128)(2,1)S(1)} collective-permute-done((bf16[64,3328]{1,0:T(8,128)(2,1)S(1)}, bf16[64,3328]{1,0:T(8,128)(2,1)S(1)}, u32[]{:S(2)}, u32[]{:S(2)}) %collective-permute-start.10) | collective-permute-done | bytes 426016 | tf_op jit(solution)/shard_map/ppermute | solution.py:41
  58.4 3.4 %collective-permute-done.8.refs_2_ = bf16[96,2048]{1,0:T(8,128)(2,1)S(1)} collective-permute-done((bf16[96,2048]{1,0:T(8,128)(2,1)S(1)}, bf16[96,2048]{1,0:T(8,128)(2,1)S(1)}, u32[]{:S(2)}, u32[]{:S(2)}) %collective-permute-start.8) | collective-permute-done | bytes 393248 | tf_op jit(solution)/shard_map/ppermute | solution.py:41
  65.4 2.3 %collective-permute-done.12.refs_2_ = bf16[768,2048]{1,0:T(8,128)(2,1)S(1)} collective-permute-done((bf16[768,2048]{1,0:T(8,128)(2,1)S(1)}, bf16[768,2048]{1,0:T(8,128)(2,1)S(1)}, u32[]{:S(2)}, u32[]{:S(2)}) %collective-permute-start.12) | collective-permute-done | bytes 3145760 | tf_op jit(solution)/shard_map/ppermute | solution.py:41
  69.4 13.1 %project.5 = (bf16[64,3328]{1,0:T(8,128)(2,1)S(1)}, bf16[64,3328]{1,0:T(8,128)(2,1)S(1)}, bf16[128,3328]{1,0:T(8,128)(2,1)S(1)}, bf16[128,3328]{1,0:T(8,128)(2,1...) custom-call(s32[2]{0:T(128)S(1)} %pad_add_fusion.refs_0_, bf16[768,2048]{1,0:T(8,128)(2,1)} %copy-done.12, ...), custom_call_target="tpu_custom_call" | custom-call | flops 13958643712 | bytes 1 | tf_op jit(solution)/shard_map/project/pallas_call | solution.py:95
  82.5 2.3 %collective-permute-done.13.refs_1_ = bf16[128,3328]{1,0:T(8,128)(2,1)S(1)} collective-permute-done((bf16[128,3328]{1,0:T(8,128)(2,1)S(1)}, bf16[128,3328]{1,0:T(8,128)(2,1)S(1)}, u32[]{:S(2)}, u32[]{:S(2)}) %collective-permute-start.13) | collective-permute-done | bytes 852000 | tf_op jit(solution)/shard_map/ppermute | solution.py:41
  85.4 4.0 %collective-permute-start.22 = (bf16[64,3328]{1,0:T(8,128)(2,1)S(1)}, bf16[64,3328]{1,0:T(8,128)(2,1)S(1)}, u32[]{:S(2)}, u32[]{:S(2)}) collective-permute-start(bf16[64,3328]{1,0:T(8,128)(2,1)S(1)} %get-tuple-element.124), channel_id=1, source_target_pairs={{0,16},{1,17},{2,18},{3,19},{16,0},{17,1},{18,2},{19,3},{32,48},{3... | collective-permute-start | bytes 1277960 | tf_op jit(solution)/shard_map/ppermute | solution.py:41
  92.6 12.9 %project.6 = (bf16[256,3328]{1,0:T(8,128)(2,1)S(1)}, bf16[256,3328]{1,0:T(8,128)(2,1)}, f32[8,128]{1,0:T(8,128)S(1)}) custom-call(s32[2]{0:T(128)S(1)} %pad_add_fusion.refs_0_, bf16[768,2048]{1,0:T(8,128)(2,1)} %copy-done.12, bf16[768,2048]{1,0:T(8,128)(2,1)} %copy-done.14, bf16[13,2048,256]{2,1,0:T(8,128)(2,1)} %get-tuple-element.89.refs_3_, ...), custom_call_target="tpu_custom_call" | custom-call | flops 13958643712 | bytes 1 | tf_op jit(solution)/shard_map/project/pallas_call | solution.py:95
  106.6 2.9 %collective-permute-start.21 = (bf16[128,3328]{1,0:T(8,128)(2,1)S(1)}, bf16[128,3328]{1,0:T(8,128)(2,1)S(1)}, u32[]{:S(2)}, u32[]{:S(2)}) collective-permute-start(bf16[128,3328]{1,0:T(8,128)(2,1)S(1)} %get-tuple-element.122), channel_id=1, source_target_pairs={{0,96},{1,97},{2,98},{3,99},{16,112},{17,113},{18,114},{19,115},{3... | collective-permute-start | bytes 2555912 | tf_op jit(solution)/shard_map/ppermute | solution.py:41
  109.5 13.2 %project.7 = (bf16[64,3328]{1,0:T(8,128)(2,1)S(1)}, bf16[64,3328]{1,0:T(8,128)(2,1)S(1)}, bf16[128,3328]{1,0:T(8,128)(2,1)S(1)}, bf16[128,3328]{1,0:T(8,128)(2,1...) custom-call(s32[2]{0:T(128)S(1)} %pad_add_fusion.refs_0_, bf16[768,2048]{1,0:T(8,128)(2,1)} %copy-done.12, ...), custom_call_target="tpu_custom_call" | custom-call | flops 13958643712 | bytes 1 | tf_op jit(solution)/shard_map/project/pallas_call | solution.py:95
  122.7 3.2 %collective-permute-start.19 = (bf16[64,3328]{1,0:T(8,128)(2,1)S(1)}, bf16[64,3328]{1,0:T(8,128)(2,1)S(1)}, u32[]{:S(2)}, u32[]{:S(2)}) collective-permute-start(bf16[64,3328]{1,0:T(8,128)(2,1)S(1)} %get-tuple-element.119), channel_id=1, source_target_pairs={{0,96},{1,97},{2,98},{3,99},{16,112},{17,113},{18,114},{19,115},{3... | collective-permute-start | bytes 1277960 | tf_op jit(solution)/shard_map/ppermute | solution.py:41
  126.0 1.8 finish.4
  130.0 6.3 %collective-permute-done.18.refs_1_ = bf16[64,3328]{1,0:T(8,128)(2,1)S(1)} collective-permute-done((bf16[64,3328]{1,0:T(8,128)(2,1)S(1)}, bf16[64,3328]{1,0:T(8,128)(2,1)S(1)}, u32[]{:S(2)}, u32[]{:S(2)}) %collective-permute-start.18) | collective-permute-done | bytes 426016 | tf_op jit(solution)/shard_map/ppermute | solution.py:41
  136.8 3.2 %collective-permute-start.26 = (bf16[128,3328]{1,0:T(8,128)(2,1)S(1)}, bf16[128,3328]{1,0:T(8,128)(2,1)S(1)}, u32[]{:S(2)}, u32[]{:S(2)}) collective-permute-start(bf16[128,3328]{1,0:T(8,128)(2,1)S(1)} %get-tuple-element.136), channel_id=1, source_target_pairs={{0,96},{1,97},{2,98},{3,99},{16,112},{17,113},{18,114},{19,115},{3... | collective-permute-start | bytes 2555912 | tf_op jit(solution)/shard_map/ppermute | solution.py:41
  140.0 3.2 %collective-permute-start.27 = (bf16[64,3328]{1,0:T(8,128)(2,1)S(1)}, bf16[64,3328]{1,0:T(8,128)(2,1)S(1)}, u32[]{:S(2)}, u32[]{:S(2)}) collective-permute-start(bf16[64,3328]{1,0:T(8,128)(2,1)S(1)} %get-tuple-element.138), channel_id=1, source_target_pairs={{0,16},{1,17},{2,18},{3,19},{16,0},{17,1},{18,2},{19,3},{32,48},{3... | collective-permute-start | bytes 1277960 | tf_op jit(solution)/shard_map/ppermute | solution.py:41
  143.2 4.0 %collective-permute-done.15.refs_1_ = bf16[256,3328]{1,0:T(8,128)(2,1)S(1)} collective-permute-done((bf16[256,3328]{1,0:T(8,128)(2,1)S(1)}, bf16[256,3328]{1,0:T(8,128)(2,1)S(1)}, u32[]{:S(2)}, u32[]{:S(2)}) %collective-permute-start.15) | collective-permute-done | bytes 1703968 | tf_op jit(solution)/shard_map/ppermute | solution.py:41
  148.5 2.9 %collective-permute-start.24 = (bf16[32,3328]{1,0:T(8,128)(2,1)S(1)}, bf16[32,3328]{1,0:T(8,128)(2,1)S(1)}, u32[]{:S(2)}, u32[]{:S(2)}) collective-permute-start(bf16[32,3328]{1,0:T(8,128)(2,1)S(1)} %get-tuple-element.133), channel_id=1, source_target_pairs={{0,96},{1,97},{2,98},{3,99},{16,112},{17,113},{18,114},{19,115},{3... | collective-permute-start | bytes 638984 | tf_op jit(solution)/shard_map/ppermute | solution.py:41
  151.4 2.8 %collective-permute-done.27.refs_4_ = bf16[64,3328]{1,0:T(8,128)(2,1)S(1)} collective-permute-done((bf16[64,3328]{1,0:T(8,128)(2,1)S(1)}, bf16[64,3328]{1,0:T(8,128)(2,1)S(1)}, u32[]{:S(2)}, u32[]{:S(2)}) %collective-permute-start.27) | collective-permute-done | bytes 426016 | tf_op jit(solution)/shard_map/ppermute | solution.py:41
  154.2 1.9 finish.5
  156.0 3.0 %collective-permute-done.25.refs_1_ = bf16[128,3328]{1,0:T(8,128)(2,1)S(1)} collective-permute-done((bf16[128,3328]{1,0:T(8,128)(2,1)S(1)}, bf16[128,3328]{1,0:T(8,128)(2,1)S(1)}, u32[]{:S(2)}, u32[]{:S(2)}) %collective-permute-start.25) | collective-permute-done | bytes 852000 | tf_op jit(solution)/shard_map/ppermute | solution.py:41
  159.7 3.2 %collective-permute-start.30 = (bf16[64,3328]{1,0:T(8,128)(2,1)S(1)}, bf16[64,3328]{1,0:T(8,128)(2,1)S(1)}, u32[]{:S(2)}, u32[]{:S(2)}) collective-permute-start(bf16[64,3328]{1,0:T(8,128)(2,1)S(1)} %get-tuple-element.147), channel_id=1, source_target_pairs={{0,16},{1,17},{2,18},{3,19},{16,0},{17,1},{18,2},{19,3},{32,48},{3... | collective-permute-start | bytes 1277960 | tf_op jit(solution)/shard_map/ppermute | solution.py:41
  164.3 2.1 %collective-permute-start.29 = (bf16[64,3328]{1,0:T(8,128)(2,1)S(1)}, bf16[64,3328]{1,0:T(8,128)(2,1)S(1)}, u32[]{:S(2)}, u32[]{:S(2)}) collective-permute-start(bf16[64,3328]{1,0:T(8,128)(2,1)S(1)} %get-tuple-element.145), channel_id=1, source_target_pairs={{0,96},{1,97},{2,98},{3,99},{16,112},{17,113},{18,114},{19,115},{3... | collective-permute-start | bytes 1277960 | tf_op jit(solution)/shard_map/ppermute | solution.py:41
  166.4 3.0 %collective-permute-done.30.refs_4_ = bf16[64,3328]{1,0:T(8,128)(2,1)S(1)} collective-permute-done((bf16[64,3328]{1,0:T(8,128)(2,1)S(1)}, bf16[64,3328]{1,0:T(8,128)(2,1)S(1)}, u32[]{:S(2)}, u32[]{:S(2)}) %collective-permute-start.30) | collective-permute-done | bytes 426016 | tf_op jit(solution)/shard_map/ppermute | solution.py:41
  169.4 1.9 finish.6
  172.6 1.9 finish.7
  174.4 15.0 %all_to_all.5 = bf16[8,8,3328]{2,1,0:T(8,128)(2,1)S(1)} all-to-all(bf16[8,8,3328]{2,1,0:T(8,128)(2,1)S(1)} %bitcast.11), channel_id=1, replica_groups=mesh['row'=8,'col'=16] {'row'}, dimensions={0} | all-to-all | bytes 851968 | tf_op jit(solution)/shard_map/all_to_all | solution.py:542
  (90 shorter events, 31.5 us)
Async XLA Ops:
  3.0 6.4 %collective-permute-start.1 = (bf16[32,2048]{1,0:T(8,128)(2,1)S(1)}, bf16[32,2048]{1,0:T(8,128)(2,1)S(1)}, u32[]{:S(2)}, u32[]{:S(2)}) collective-permute-start(bf16[32,2048]{1,0:T(8,128)(2,1)S(1)} %get-tuple-element.81.refs_0_), channel_id=1, source_target_pairs={{0,2},{1,3},{2,0},{3,1},{16,18},{17,19},{18,16},{19,17},{32,34},{3... | collective-permute-start | bytes 393224 | tf_op jit(solution)/shard_map/ppermute | solution.py:41
  5.1 20.8 %collective-permute-start = (bf16[96,2048]{1,0:T(8,128)(2,1)S(1)}, bf16[96,2048]{1,0:T(8,128)(2,1)S(1)}, u32[]{:S(2)}, u32[]{:S(2)}) collective-permute-start(bf16[96,2048]{1,0:T(8,128)(2,1)S(1)} %get-tuple-element.79.refs_0_), channel_id=1, source_target_pairs={{0,2},{1,3},{2,0},{3,1},{16,18},{17,19},{18,16},{19,17},{32,34},{3... | collective-permute-start | bytes 1179656 | tf_op jit(solution)/shard_map/ppermute | solution.py:41
  9.5 16.5 %collective-permute-start.6 = (bf16[64,2048]{1,0:T(8,128)(2,1)S(1)}, bf16[64,2048]{1,0:T(8,128)(2,1)S(1)}, u32[]{:S(2)}, u32[]{:S(2)}) collective-permute-start(bf16[64,2048]{1,0:T(8,128)(2,1)S(1)} %get-tuple-element.86.refs_0_), channel_id=1, source_target_pairs={{0,4},{1,5},{2,6},{3,7},{16,20},{17,21},{18,22},{19,23},{32,36},{3... | collective-permute-start | bytes 786440 | tf_op jit(solution)/shard_map/ppermute | solution.py:41
  11.1 14.8 %collective-permute-start.5 = (bf16[64,2048]{1,0:T(8,128)(2,1)S(1)}, bf16[64,2048]{1,0:T(8,128)(2,1)S(1)}, u32[]{:S(2)}, u32[]{:S(2)}) collective-permute-start(bf16[64,2048]{1,0:T(8,128)(2,1)S(1)} %get-tuple-element.86.refs_0_), channel_id=1, source_target_pairs={{0,8},{1,9},{2,10},{3,11},{16,24},{17,25},{18,26},{19,27},{32,40},... | collective-permute-start | bytes 786440 | tf_op jit(solution)/shard_map/ppermute | solution.py:41
  13.9 12.1 %collective-permute-start.4 = (bf16[64,2048]{1,0:T(8,128)(2,1)S(1)}, bf16[64,2048]{1,0:T(8,128)(2,1)S(1)}, u32[]{:S(2)}, u32[]{:S(2)}) collective-permute-start(bf16[64,2048]{1,0:T(8,128)(2,1)S(1)} %get-tuple-element.86.refs_0_), channel_id=1, source_target_pairs={{0,12},{1,13},{2,14},{3,15},{16,28},{17,29},{18,30},{19,31},{32,44... | collective-permute-start | bytes 786440 | tf_op jit(solution)/shard_map/ppermute | solution.py:41
  26.1 3.4 %collective-permute-start.7 = (bf16[256,2048]{1,0:T(8,128)(2,1)S(1)}, bf16[256,2048]{1,0:T(8,128)(2,1)S(1)}, u32[]{:S(2)}, u32[]{:S(2)}) collective-permute-start(bf16[256,2048]{1,0:T(8,128)(2,1)S(1)} %get-tuple-element.88.refs_1_), channel_id=1, source_target_pairs={{0,1},{1,0},{2,3},{3,2},{16,17},{17,16},{18,19},{19,18},{32,33},{3... | collective-permute-start | bytes 3145736 | tf_op jit(solution)/shard_map/ppermute | solution.py:41
  26.3 21.1 %collective-permute-start.3 = (bf16[192,2048]{1,0:T(8,128)(2,1)S(1)}, bf16[192,2048]{1,0:T(8,128)(2,1)S(1)}, u32[]{:S(2)}, u32[]{:S(2)}) collective-permute-start(bf16[192,2048]{1,0:T(8,128)(2,1)S(1)} %get-tuple-element.85.refs_0_), channel_id=1, source_target_pairs={{0,4},{1,5},{2,6},{3,7},{16,20},{17,21},{18,22},{19,23},{32,36},{3... | collective-permute-start | bytes 2359304 | tf_op jit(solution)/shard_map/ppermute | solution.py:41
  26.9 20.6 %collective-permute-start.2 = (bf16[192,2048]{1,0:T(8,128)(2,1)S(1)}, bf16[192,2048]{1,0:T(8,128)(2,1)S(1)}, u32[]{:S(2)}, u32[]{:S(2)}) collective-permute-start(bf16[192,2048]{1,0:T(8,128)(2,1)S(1)} %get-tuple-element.85.refs_0_), channel_id=1, source_target_pairs={{0,12},{1,13},{2,14},{3,15},{16,28},{17,29},{18,30},{19,31},{32,44... | collective-permute-start | bytes 2359304 | tf_op jit(solution)/shard_map/ppermute | solution.py:41
  43.6 13.0 %collective-permute-start.10 = (bf16[64,3328]{1,0:T(8,128)(2,1)S(1)}, bf16[64,3328]{1,0:T(8,128)(2,1)S(1)}, u32[]{:S(2)}, u32[]{:S(2)}) collective-permute-start(bf16[64,3328]{1,0:T(8,128)(2,1)S(1)} %get-tuple-element.96), channel_id=1, source_target_pairs={{0,32},{1,33},{2,34},{3,35},{16,48},{17,49},{18,50},{19,51},{32,64... | collective-permute-start | bytes 1277960 | tf_op jit(solution)/shard_map/ppermute | solution.py:41
  45.3 11.4 %collective-permute-start.11 = (bf16[64,3328]{1,0:T(8,128)(2,1)S(1)}, bf16[64,3328]{1,0:T(8,128)(2,1)S(1)}, u32[]{:S(2)}, u32[]{:S(2)}) collective-permute-start(bf16[64,3328]{1,0:T(8,128)(2,1)S(1)} %get-tuple-element.98), channel_id=1, source_target_pairs={{0,96},{1,97},{2,98},{3,99},{16,112},{17,113},{18,114},{19,115},{3... | collective-permute-start | bytes 1277960 | tf_op jit(solution)/shard_map/ppermute | solution.py:41
  47.5 10.9 %collective-permute-start.9 = (bf16[96,2048]{1,0:T(8,128)(2,1)S(1)}, bf16[96,2048]{1,0:T(8,128)(2,1)S(1)}, u32[]{:S(2)}, u32[]{:S(2)}) collective-permute-start(bf16[96,2048]{1,0:T(8,128)(2,1)S(1)} %get-tuple-element.94), channel_id=1, source_target_pairs={{0,12},{1,13},{2,14},{3,15},{16,28},{17,29},{18,30},{19,31},{32,44... | collective-permute-start | bytes 1179656 | tf_op jit(solution)/shard_map/ppermute | solution.py:41
  50.5 11.3 %collective-permute-start.8 = (bf16[96,2048]{1,0:T(8,128)(2,1)S(1)}, bf16[96,2048]{1,0:T(8,128)(2,1)S(1)}, u32[]{:S(2)}, u32[]{:S(2)}) collective-permute-start(bf16[96,2048]{1,0:T(8,128)(2,1)S(1)} %get-tuple-element.92), channel_id=1, source_target_pairs={{0,4},{1,5},{2,6},{3,7},{16,20},{17,21},{18,22},{19,23},{32,36},{3... | collective-permute-start | bytes 1179656 | tf_op jit(solution)/shard_map/ppermute | solution.py:41
  62.0 5.7 %collective-permute-start.12 = (bf16[768,2048]{1,0:T(8,128)(2,1)S(1)}, bf16[768,2048]{1,0:T(8,128)(2,1)S(1)}, u32[]{:S(2)}, u32[]{:S(2)}) collective-permute-start(bf16[768,2048]{1,0:T(8,128)(2,1)S(1)} %get-tuple-element.101.refs_1_), channel_id=1, source_target_pairs={{0,1},{1,0},{2,3},{3,2},{16,17},{17,16},{18,19},{19,18},{32,33},{3... | collective-permute-start | bytes 9437192 | tf_op jit(solution)/shard_map/ppermute | solution.py:41
  62.1 22.6 %collective-permute-start.13 = (bf16[128,3328]{1,0:T(8,128)(2,1)S(1)}, bf16[128,3328]{1,0:T(8,128)(2,1)S(1)}, u32[]{:S(2)}, u32[]{:S(2)}) collective-permute-start(bf16[128,3328]{1,0:T(8,128)(2,1)S(1)} %get-tuple-element.103), channel_id=1, source_target_pairs={{0,32},{1,33},{2,34},{3,35},{16,48},{17,49},{18,50},{19,51},{32,64... | collective-permute-start | bytes 2555912 | tf_op jit(solution)/shard_map/ppermute | solution.py:41
  63.8 21.0 %collective-permute-start.14 = (bf16[128,3328]{1,0:T(8,128)(2,1)S(1)}, bf16[128,3328]{1,0:T(8,128)(2,1)S(1)}, u32[]{:S(2)}, u32[]{:S(2)}) collective-permute-start(bf16[128,3328]{1,0:T(8,128)(2,1)S(1)} %get-tuple-element.104), channel_id=1, source_target_pairs={{0,96},{1,97},{2,98},{3,99},{16,112},{17,113},{18,114},{19,115},{3... | collective-permute-start | bytes 2555912 | tf_op jit(solution)/shard_map/ppermute | solution.py:41
  85.4 37.3 %collective-permute-start.22 = (bf16[64,3328]{1,0:T(8,128)(2,1)S(1)}, bf16[64,3328]{1,0:T(8,128)(2,1)S(1)}, u32[]{:S(2)}, u32[]{:S(2)}) collective-permute-start(bf16[64,3328]{1,0:T(8,128)(2,1)S(1)} %get-tuple-element.124), channel_id=1, source_target_pairs={{0,16},{1,17},{2,18},{3,19},{16,0},{17,1},{18,2},{19,3},{32,48},{3... | collective-permute-start | bytes 1277960 | tf_op jit(solution)/shard_map/ppermute | solution.py:41
  89.4 16.3 %collective-permute-start.16 = (bf16[64,3328]{1,0:T(8,128)(2,1)S(1)}, bf16[64,3328]{1,0:T(8,128)(2,1)S(1)}, u32[]{:S(2)}, u32[]{:S(2)}) collective-permute-start(bf16[64,3328]{1,0:T(8,128)(2,1)S(1)} %get-tuple-element.111), channel_id=1, source_target_pairs={{0,32},{1,33},{2,34},{3,35},{16,48},{17,49},{18,50},{19,51},{32,64... | collective-permute-start | bytes 1277960 | tf_op jit(solution)/shard_map/ppermute | solution.py:41
  91.0 14.7 %collective-permute-start.17 = (bf16[64,3328]{1,0:T(8,128)(2,1)S(1)}, bf16[64,3328]{1,0:T(8,128)(2,1)S(1)}, u32[]{:S(2)}, u32[]{:S(2)}) collective-permute-start(bf16[64,3328]{1,0:T(8,128)(2,1)S(1)} %get-tuple-element.113), channel_id=1, source_target_pairs={{0,96},{1,97},{2,98},{3,99},{16,112},{17,113},{18,114},{19,115},{3... | collective-permute-start | bytes 1277960 | tf_op jit(solution)/shard_map/ppermute | solution.py:41
  105.5 41.7 %collective-permute-start.15 = (bf16[256,3328]{1,0:T(8,128)(2,1)S(1)}, bf16[256,3328]{1,0:T(8,128)(2,1)S(1)}, u32[]{:S(2)}, u32[]{:S(2)}) collective-permute-start(bf16[256,3328]{1,0:T(8,128)(2,1)S(1)} %get-tuple-element.109), channel_id=1, source_target_pairs={{0,16},{1,17},{2,18},{3,19},{16,0},{17,1},{18,2},{19,3},{32,48},{3... | collective-permute-start | bytes 5111816 | tf_op jit(solution)/shard_map/ppermute | solution.py:41
  106.2 23.2 %collective-permute-start.20 = (bf16[128,3328]{1,0:T(8,128)(2,1)S(1)}, bf16[128,3328]{1,0:T(8,128)(2,1)S(1)}, u32[]{:S(2)}, u32[]{:S(2)}) collective-permute-start(bf16[128,3328]{1,0:T(8,128)(2,1)S(1)} %get-tuple-element.121), channel_id=1, source_target_pairs={{0,32},{1,33},{2,34},{3,35},{16,48},{17,49},{18,50},{19,51},{32,64... | collective-permute-start | bytes 2555912 | tf_op jit(solution)/shard_map/ppermute | solution.py:41
  106.6 22.7 %collective-permute-start.21 = (bf16[128,3328]{1,0:T(8,128)(2,1)S(1)}, bf16[128,3328]{1,0:T(8,128)(2,1)S(1)}, u32[]{:S(2)}, u32[]{:S(2)}) collective-permute-start(bf16[128,3328]{1,0:T(8,128)(2,1)S(1)} %get-tuple-element.122), channel_id=1, source_target_pairs={{0,96},{1,97},{2,98},{3,99},{16,112},{17,113},{18,114},{19,115},{3... | collective-permute-start | bytes 2555912 | tf_op jit(solution)/shard_map/ppermute | solution.py:41
  122.6 13.6 %collective-permute-start.18 = (bf16[64,3328]{1,0:T(8,128)(2,1)S(1)}, bf16[64,3328]{1,0:T(8,128)(2,1)S(1)}, u32[]{:S(2)}, u32[]{:S(2)}) collective-permute-start(bf16[64,3328]{1,0:T(8,128)(2,1)S(1)} %get-tuple-element.117), channel_id=1, source_target_pairs={{0,32},{1,33},{2,34},{3,35},{16,48},{17,49},{18,50},{19,51},{32,64... | collective-permute-start | bytes 1277960 | tf_op jit(solution)/shard_map/ppermute | solution.py:41
  122.7 13.5 %collective-permute-start.19 = (bf16[64,3328]{1,0:T(8,128)(2,1)S(1)}, bf16[64,3328]{1,0:T(8,128)(2,1)S(1)}, u32[]{:S(2)}, u32[]{:S(2)}) collective-permute-start(bf16[64,3328]{1,0:T(8,128)(2,1)S(1)} %get-tuple-element.119), channel_id=1, source_target_pairs={{0,96},{1,97},{2,98},{3,99},{16,112},{17,113},{18,114},{19,115},{3... | collective-permute-start | bytes 1277960 | tf_op jit(solution)/shard_map/ppermute | solution.py:41
  130.0 17.3 %copy-start.2 = (bf16[256,3328]{1,0:T(8,128)(2,1)S(1)}, bf16[256,3328]{1,0:T(8,128)(2,1)}, u32[]{:S(2)}) copy-start(bf16[256,3328]{1,0:T(8,128)(2,1)} %get-tuple-element.108.refs_0_) | copy-start | bytes 5111812
  136.7 22.3 %collective-permute-start.25 = (bf16[128,3328]{1,0:T(8,128)(2,1)S(1)}, bf16[128,3328]{1,0:T(8,128)(2,1)S(1)}, u32[]{:S(2)}, u32[]{:S(2)}) collective-permute-start(bf16[128,3328]{1,0:T(8,128)(2,1)S(1)} %get-tuple-element.135), channel_id=1, source_target_pairs={{0,32},{1,33},{2,34},{3,35},{16,48},{17,49},{18,50},{19,51},{32,64... | collective-permute-start | bytes 2555912 | tf_op jit(solution)/shard_map/ppermute | solution.py:41
  136.8 22.2 %collective-permute-start.26 = (bf16[128,3328]{1,0:T(8,128)(2,1)S(1)}, bf16[128,3328]{1,0:T(8,128)(2,1)S(1)}, u32[]{:S(2)}, u32[]{:S(2)}) collective-permute-start(bf16[128,3328]{1,0:T(8,128)(2,1)S(1)} %get-tuple-element.136), channel_id=1, source_target_pairs={{0,96},{1,97},{2,98},{3,99},{16,112},{17,113},{18,114},{19,115},{3... | collective-permute-start | bytes 2555912 | tf_op jit(solution)/shard_map/ppermute | solution.py:41
  140.0 14.1 %collective-permute-start.27 = (bf16[64,3328]{1,0:T(8,128)(2,1)S(1)}, bf16[64,3328]{1,0:T(8,128)(2,1)S(1)}, u32[]{:S(2)}, u32[]{:S(2)}) collective-permute-start(bf16[64,3328]{1,0:T(8,128)(2,1)S(1)} %get-tuple-element.138), channel_id=1, source_target_pairs={{0,16},{1,17},{2,18},{3,19},{16,0},{17,1},{18,2},{19,3},{32,48},{3... | collective-permute-start | bytes 1277960 | tf_op jit(solution)/shard_map/ppermute | solution.py:41
  148.1 14.8 %collective-permute-start.23 = (bf16[32,3328]{1,0:T(8,128)(2,1)S(1)}, bf16[32,3328]{1,0:T(8,128)(2,1)S(1)}, u32[]{:S(2)}, u32[]{:S(2)}) collective-permute-start(bf16[32,3328]{1,0:T(8,128)(2,1)S(1)} %get-tuple-element.131), channel_id=1, source_target_pairs={{0,32},{1,33},{2,34},{3,35},{16,48},{17,49},{18,50},{19,51},{32,64... | collective-permute-start | bytes 638984 | tf_op jit(solution)/shard_map/ppermute | solution.py:41
  148.5 14.3 %collective-permute-start.24 = (bf16[32,3328]{1,0:T(8,128)(2,1)S(1)}, bf16[32,3328]{1,0:T(8,128)(2,1)S(1)}, u32[]{:S(2)}, u32[]{:S(2)}) collective-permute-start(bf16[32,3328]{1,0:T(8,128)(2,1)S(1)} %get-tuple-element.133), channel_id=1, source_target_pairs={{0,96},{1,97},{2,98},{3,99},{16,112},{17,113},{18,114},{19,115},{3... | collective-permute-start | bytes 638984 | tf_op jit(solution)/shard_map/ppermute | solution.py:41
  159.7 9.7 %collective-permute-start.30 = (bf16[64,3328]{1,0:T(8,128)(2,1)S(1)}, bf16[64,3328]{1,0:T(8,128)(2,1)S(1)}, u32[]{:S(2)}, u32[]{:S(2)}) collective-permute-start(bf16[64,3328]{1,0:T(8,128)(2,1)S(1)} %get-tuple-element.147), channel_id=1, source_target_pairs={{0,16},{1,17},{2,18},{3,19},{16,0},{17,1},{18,2},{19,3},{32,48},{3... | collective-permute-start | bytes 1277960 | tf_op jit(solution)/shard_map/ppermute | solution.py:41
  163.1 9.4 %collective-permute-start.28 = (bf16[64,3328]{1,0:T(8,128)(2,1)S(1)}, bf16[64,3328]{1,0:T(8,128)(2,1)S(1)}, u32[]{:S(2)}, u32[]{:S(2)}) collective-permute-start(bf16[64,3328]{1,0:T(8,128)(2,1)S(1)} %get-tuple-element.144), channel_id=1, source_target_pairs={{0,32},{1,33},{2,34},{3,35},{16,48},{17,49},{18,50},{19,51},{32,64... | collective-permute-start | bytes 1277960 | tf_op jit(solution)/shard_map/ppermute | solution.py:41
  164.3 8.2 %collective-permute-start.29 = (bf16[64,3328]{1,0:T(8,128)(2,1)S(1)}, bf16[64,3328]{1,0:T(8,128)(2,1)S(1)}, u32[]{:S(2)}, u32[]{:S(2)}) collective-permute-start(bf16[64,3328]{1,0:T(8,128)(2,1)S(1)} %get-tuple-element.145), channel_id=1, source_target_pairs={{0,96},{1,97},{2,98},{3,99},{16,112},{17,113},{18,114},{19,115},{3... | collective-permute-start | bytes 1277960 | tf_op jit(solution)/shard_map/ppermute | solution.py:41
  (15 other events, 121.4 us)
